TPU v7x, 512 devices: a whole 4x4x16 slice. The times are simulated.
512 devices in a mesh: sec: 64 (over z, x), mpo: 8 (over y, core).
Axes of the slice: x: 4, y: 4, z: 16, core: 2. Of those that a mesh axis runs over, the one named last changes fastest.
Arguments:
- start_vector: float32 [512, 8192], P('sec'), may hold values from -6 to 6
- precond_diag: float32 [512, 8192], P('sec'), may hold values from 1 to 10
- left_env: float32 [24, 512, 8], P('mpo', 'sec'), may hold values from -2 to 2
- right_env: float32 [24, 8192, 128], P('mpo', 'sec'), may hold values from -0.109375 to 0.109375
- right_shift: int32 [24], P('mpo'), may hold values from 0 to 63
- sector_length: int32 [64], P('sec'), may hold values from 1 to 8, 384 in all
Outputs:
- basis_three: float32 [512, 8192], P('sec', 'mpo')
- image_three: float32 [512, 8192], P('sec', 'mpo')
Inputs may be any that keep to these rules, and one draw needn't show every extreme that they name: `sector_length`: each sector has 1 to 8 live rows, and some sector has exactly 8; they add up to 384.
All inputs are finite; a program needn't handle non-finite values. No bound on the sum of `sector_length` on one device may be relied on, other than what follows from the above.
Results may differ from a plain program's by a relative error of at most 0.0003.
Values sent between devices are 32-bit elements; how exact they have to be, the bound alone decides.
A program may use at most 64 MiB of HBM per device.

v0:
```python
import jax
import jax.numpy as jnp
from jax import lax
from jax.sharding import PartitionSpec as P

BR = 128


epsilon = 1e-06


def inner_sum(left, right):
    return jnp.sum(left * right)


def per_device(start_vector, precond_diag, left_env, right_env, right_shift, sector_length):
    row_count, col_count = start_vector.shape
    sectors = lax.axis_size("sec")
    groups = lax.axis_size("mpo")
    cells = jnp.float32(row_count * sectors * col_count)
    block_count = col_count // BR
    live = (lax.iota(jnp.int32, row_count) < sector_length[0]).astype(jnp.float32)[:, None]
    gathered = lax.all_gather(right_env, "sec", axis=1, tiled=True)
    right_blocks = gathered.reshape(gathered.shape[0], block_count, BR, BR)

    def local_image(vector):
        summed = jnp.zeros((row_count, col_count), jnp.float32)
        for term_index in range(left_env.shape[0]):
            mixed = jnp.dot(
                left_env[term_index],
                vector,
                precision=lax.Precision.HIGHEST,
                preferred_element_type=jnp.float32,
            )
            mixed = jnp.roll(
                mixed.reshape(row_count, block_count, BR), -right_shift[term_index], axis=1
            )
            result = jnp.einsum(
                "inb,nbc->inc", mixed, right_blocks[term_index], precision=lax.Precision.HIGHEST
            )
            summed = summed + result.reshape(row_count, col_count)
        return summed * live

    def apply_operator(vector):
        return lax.psum(local_image(vector), "mpo")

    def global_sums(values):
        return lax.psum(values, "sec")

    def finish(array):
        share_width = col_count // groups
        return lax.dynamic_slice_in_dim(array, lax.axis_index("mpo") * share_width, share_width, 1)

    def orthonormal(correction, basis):
        count = len(basis)
        sums = global_sums(tuple((inner_sum(member, correction) for member in basis)))
        update = correction
        for index in range(count):
            update = update - sums[index] / cells * basis[index]
        squared = global_sums((inner_sum(update, update),))[0]
        return update * jnp.sqrt(cells / (squared + epsilon))

    masked = start_vector * live
    norm_sum = global_sums((inner_sum(masked, masked),))[0]
    factor = jnp.sqrt(cells / (norm_sum + epsilon))
    basis_one = masked * factor
    image_one = apply_operator(basis_one)
    rayleigh = global_sums((inner_sum(basis_one, image_one),))[0] / cells
    correction = (image_one - rayleigh * basis_one) / precond_diag
    basis_two = orthonormal(correction, [basis_one])
    image_two = apply_operator(basis_two)
    cross_one, cross_two, diagonal_two = global_sums(
        (
            inner_sum(basis_one, image_two),
            inner_sum(basis_two, image_one),
            inner_sum(basis_two, image_two),
        )
    )
    coupling = (cross_one + cross_two) / (2.0 * cells)
    second = diagonal_two / cells
    half_gap = (rayleigh - second) / 2.0
    ritz_value = (rayleigh + second) / 2.0 - jnp.sqrt(half_gap * half_gap + coupling * coupling)
    rotation = jnp.arctan2(coupling, half_gap) / 2.0
    weight_one = -jnp.sin(rotation)
    weight_two = jnp.cos(rotation)
    ritz_vector = weight_one * basis_one + weight_two * basis_two
    ritz_image = weight_one * image_one + weight_two * image_two
    correction_two = (ritz_image - ritz_value * ritz_vector) / precond_diag
    basis_three = orthonormal(correction_two, [basis_one, basis_two])
    image_three = apply_operator(basis_three)
    return (finish(basis_three), finish(image_three))


def solution(mesh):
    placed = (
        P("sec", None),
        P("sec", None),
        P("mpo", "sec", None),
        P("mpo", "sec", None),
        P("mpo"),
        P("sec"),
    )
    return jax.shard_map(
        per_device,
        mesh=mesh,
        in_specs=placed,
        out_specs=(P("sec", "mpo"), P("sec", "mpo")),
        check_vma=False,
    )
```

profile of v0, /device:TPU:1, one launch (start us, length us, event | category | flops | bytes accessed | tf_op | source)
XLA Modules:
  0.0 1319.6 jit_solution(1160985384237475418)
XLA Ops:
  7.2 0.0 all-gather.2.cloned.1.call-start
  7.2 0.7 all-gather.2.cloned.1.call-update
  7.9 0.0 all-reduce.6.cloned.1.call-start
  8.6 1.7 multiply_reduce_fusion.9
  10.3 124.1 %psum.91 = f32[]{:T(128)} all-reduce(f32[]{:T(128)} %multiply_reduce_fusion.9), channel_id=1, replica_groups=mesh['sec'=64,'mpo'=8] {'sec'}, use_global_device_ids=true, to_apply=%region_1.0 | all-reduce | flops 1 | bytes 8 | tf_op jit(solution)/shard_map/psum | solution.py:48
  134.4 1.4 fusion.70
  138.5 1.4 convolution_bitcast_fusion.8
  139.9 1.4 convolution_bitcast_fusion.7
  141.3 1.4 convolution_bitcast_fusion.6
  142.7 43.4 %all-gather.2.cloned.1.call-done = f32[3,8192,128]{2,1,0:T(8,128)} async-done(((f32[3,128,128]{2,1,0:T(8,128)}), f32[3,8192,128]{2,1,0:T(8,128)}) %all-gather.2.cloned.1.call-update) | async-done | bytes 12582928 | tf_op jit(solution)/shard_map/all_gather | solution.py:23
  186.1 8.7 fusion.69
  194.8 0.0 copy-start
  194.8 6.8 fusion.25
  201.6 0.0 copy-start.8
  201.6 3.6 convolution_add_fusion.5
  205.2 0.0 copy-done
  205.3 0.0 copy-done.3
  205.3 4.3 fusion.5
  209.6 0.0 all-reduce.6.cloned.1.call-update
  209.6 0.0 all-reduce.8.cloned.1.call-start
  209.7 70.8 %all-reduce.6.cloned.1.call-done = f32[8,8192]{1,0:T(8,128)} async-done(((f32[8,8192]{1,0:T(8,128)}), f32[8,8192]{1,0:T(8,128)}) %all-reduce.6.cloned.1.call-update) | async-done | bytes 262160 | tf_op jit(solution)/shard_map/psum | solution.py:45
  280.4 0.0 copy-done.6
  280.4 1.7 multiply_reduce_fusion.8
  282.1 116.6 %psum.93 = f32[]{:T(128)} all-reduce(f32[]{:T(128)} %multiply_reduce_fusion.8), channel_id=1, replica_groups=mesh['sec'=64,'mpo'=8] {'sec'}, use_global_device_ids=true, to_apply=%region_4.6 | all-reduce | flops 1 | bytes 8 | tf_op jit(solution)/shard_map/psum | solution.py:48
  399.4 0.0 copy-done.8
  399.4 1.7 multiply_reduce_fusion.7
  401.1 110.8 %psum.94 = f32[]{:T(128)} all-reduce(f32[]{:T(128)} %multiply_reduce_fusion.7), channel_id=1, replica_groups=mesh['sec'=64,'mpo'=8] {'sec'}, use_global_device_ids=true, to_apply=%region_6.8 | all-reduce | flops 1 | bytes 8 | tf_op jit(solution)/shard_map/psum | solution.py:48
  512.5 1.7 multiply_reduce_fusion.6
  514.2 113.4 %psum.95 = f32[]{:T(128)} all-reduce(f32[]{:T(128)} %get-tuple-element.15), channel_id=1, replica_groups=mesh['sec'=64,'mpo'=8] {'sec'}, use_global_device_ids=true, to_apply=%region_8.10 | all-reduce | flops 1 | bytes 8 | tf_op jit(solution)/shard_map/psum | solution.py:48
  628.3 0.0 copy-start.1
  628.3 0.0 copy-done.9
  628.3 0.3 convolution_bitcast_fusion.5
  628.7 0.3 convolution_bitcast_fusion.4
  629.0 0.3 convolution_bitcast_fusion.3
  629.4 0.0 copy-start.4
  629.4 5.5 fusion.18
  634.9 0.0 copy-done.1
  634.9 3.6 convolution_add_fusion.3
  638.5 0.0 copy-done.4
  638.5 4.3 fusion.3
  642.8 0.0 all-reduce.8.cloned.1.call-update
  642.8 0.0 all-reduce.10.cloned.1.call-start
  642.9 151.7 %all-reduce.8.cloned.1.call-done = f32[8,8192]{1,0:T(8,128)} async-done(((f32[8,8192]{1,0:T(8,128)}), f32[8,8192]{1,0:T(8,128)}) %all-reduce.8.cloned.1.call-update) | async-done | bytes 262160 | tf_op jit(solution)/shard_map/psum | solution.py:45
  794.6 0.0 copy-done.7
  794.6 1.7 multiply_reduce_fusion.4
  797.5 116.6 %all-reduce.1 = (f32[]{:T(128)}, f32[]{:T(128)}) all-reduce(f32[]{:T(128)} %get-tuple-element.6, f32[]{:T(128)S(6)} %add.114), channel_id=1, replica_groups=mesh['sec'=64,'mpo'=8] {'sec'}, use_global_device_ids=true, to_apply=%region_15.17 | all-reduce | flops 2 | bytes 16 | tf_op jit(solution)/shard_map/psum | solution.py:48
  916.8 1.7 multiply_reduce_fusion.2
  918.5 111.5 %all-reduce = (f32[]{:T(128)}, f32[]{:T(128)}) all-reduce(f32[]{:T(128)} %get-tuple-element.4, f32[]{:T(128)} %get-tuple-element.3), channel_id=1, replica_groups=mesh['sec'=64,'mpo'=8] {'sec'}, use_global_device_ids=true, to_apply=%region_19.21 | all-reduce | flops 2 | bytes 16 | tf_op jit(solution)/shard_map/psum | solution.py:48
  1031.3 0.7 multiply_reduce_fusion
  1032.0 113.4 %psum.102 = f32[]{:T(128)} all-reduce(f32[]{:T(128)} %get-tuple-element.12), channel_id=1, replica_groups=mesh['sec'=64,'mpo'=8] {'sec'}, use_global_device_ids=true, to_apply=%region_21.23 | all-reduce | flops 1 | bytes 8 | tf_op jit(solution)/shard_map/psum | solution.py:48
  1146.2 0.0 copy-start.2
  1146.2 0.3 convolution_bitcast_fusion.2
  1146.6 0.3 convolution_bitcast_fusion.1
  1146.9 0.3 convolution_bitcast_fusion
  1147.3 0.0 copy-start.5
  1147.3 5.4 fusion.11
  1152.8 0.0 copy-done.2
  1152.8 3.6 convolution_add_fusion.1
  1156.4 0.0 copy-done.5
  1156.4 4.3 fusion.1
  1160.7 0.0 all-reduce.10.cloned.1.call-update
  1160.7 0.6 constant_dynamic-slice_fusion.1
  1161.4 150.3 %all-reduce.10.cloned.1.call-done = f32[8,8192]{1,0:T(8,128)} async-done(((f32[8,8192]{1,0:T(8,128)}), f32[8,8192]{1,0:T(8,128)}) %all-reduce.10.cloned.1.call-update) | async-done | bytes 262160 | tf_op jit(solution)/shard_map/psum | solution.py:45
  1311.7 1.4 constant_dynamic-slice_fusion
  (6 shorter events, 0.0 us)
Async XLA Ops:
  7.2 179.0 %all-gather.2.cloned.1.call-start = ((), (), s32[]{:S(2)}) async-start(), calls=%async_computation | async-start | bytes 12779520 | tf_op jit(solution)/shard_map/all_gather | solution.py:23
  7.9 272.5 %all-reduce.6.cloned.1.call-start = ((), (), s32[]{:S(2)}) async-start(), calls=%async_computation.1 | async-start | bytes 524288 | tf_op jit(solution)/shard_map/psum | solution.py:45
  194.8 10.5 copy-start
  194.8 10.5 copy-start.3
  201.6 78.8 %copy-start.6 = (f32[8,8192]{1,0:T(8,128)S(1)}, f32[8,8192]{1,0:T(8,128)}, u32[]{:S(2)}) copy-start(f32[8,8192]{1,0:T(8,128)} %param.8) | copy-start | bytes 786436
  201.6 197.8 %copy-start.8 = (f32[8,8192]{1,0:T(8,128)S(1)}, f32[8,8192]{1,0:T(8,128)}, u32[]{:S(2)}) copy-start(f32[8,8192]{1,0:T(8,128)} %param.9) | copy-start | bytes 786436
  205.3 423.1 %copy-start.9 = (f32[3,8,8]{2,1,0:T(8,128)S(1)}, f32[3,8,8]{2,1,0:T(8,128)}, u32[]{:S(2)}) copy-start(f32[3,8,8]{2,1,0:T(8,128)} %param.10) | copy-start | bytes 2308
  209.6 585.0 %all-reduce.8.cloned.1.call-start = ((), (), s32[]{:S(2)}) async-start(), calls=%async_computation.2 | async-start | bytes 524288 | tf_op jit(solution)/shard_map/psum | solution.py:45
  628.3 6.6 copy-start.1
  629.4 9.1 copy-start.4
  634.9 159.7 %copy-start.7 = (f32[8,8192]{1,0:T(8,128)S(1)}, f32[8,8192]{1,0:T(8,128)}, u32[]{:S(2)}) copy-start(f32[8,8192]{1,0:T(8,128)} %all-reduce.6.cloned.1.call-done) | copy-start | bytes 786436
  642.8 668.8 %all-reduce.10.cloned.1.call-start = ((), (), s32[]{:S(2)}) async-start(), calls=%async_computation.3 | async-start | bytes 524288 | tf_op jit(solution)/shard_map/psum | solution.py:45
  1146.2 6.6 copy-start.2
  1147.3 9.1 copy-start.5
Sparse Core Ops, SparseCore 0:
  11.0 175.1 all-gather.1
  209.7 70.6 all-reduce.5
  643.0 151.5 all-reduce.7
  1160.8 150.7 all-reduce.9
where the time goes:
time: 1320 us
  blocking collectives  806 us (61%)
  waiting for transfers between devices  417 us (32%)
  matrix products  47.8 us (4%)
  between operations  25.2 us (2%)
    psum x7, blocking collectives, global_sums(): return lax.psum(values, 'sec')  806 us
    psum x3, waiting for transfers between devices, apply_operator(): return lax.psum(local_image(vector), 'mpo')  373 us
    all_gather x1, waiting for transfers between devices, per_device(): gathered = lax.all_gather(right_env, 'sec', axis=1, tiled=True)  43.4 us
    dot_general x9, matrix products, local_image(): jnp.einsum('inb,nbc->inc', mixed, right_blocks[term_index], precision=lax...  41.5 us
  transfers between devices with their start and end apart: 4, of which 4 were waited for; matrix products, arithmetic and copies ran while one was open for 1% of the time, Pallas kernels for 0%

commit v1 on v0

v1 whole, which is shorter than its diff:
```python
import functools

import jax
import jax.numpy as jnp
from jax import lax
from jax.experimental import pallas as pl
from jax.experimental.pallas import tpu as pltpu
from jax.sharding import PartitionSpec as P

MESH = pl.DeviceIdType.MESH
F32 = jnp.float32
BF16 = jnp.bfloat16

NX, NY, NZ = 4, 4, 16
ROWS, BR, NBLK = 8, 128, 64
TPD = 3
KS = 4
CELLS = float(512 * 8192)
EPS = 1e-6


def kernel(
    start_ref,
    diag_ref,
    left_ref,
    right_ref,
    shift_ref,
    length_ref,
    basis_ref,
    image_ref,
    rbuf,
    r_hi,
    r_lo,
    v1,
    v2,
    v3,
    y_own,
    y_in1,
    y_in2,
    y_in3,
    piece,
    src_gd,
    got_gd,
    left_tile,
    left_row,
    left_all,
    shift_tile,
    shift_all,
    shift_sm,
    left_wide,
    mask,
    dz,
    dp,
    dc,
    out_src,
    out_got,
    w_send,
    w_recv,
    ag_send,
    ag_plus,
    ag_minus,
    ag_core,
    y_send,
    y_recv,
    dot_send,
    dot_recv,
    st_send,
    st_recv,
    sm_sem,
    out_send,
    out_recv,
):
    sec = lax.axis_index("sec")
    mpo = lax.axis_index("mpo")
    z, x = lax.div(sec, 4), lax.rem(sec, 4)
    y, c = lax.div(mpo, 2), lax.rem(mpo, 2)

    def dev(xx, yy, zz, cc):
        return (zz * 4 + xx, yy * 2 + cc)

    def send(src, dst, send_sem, recv_sem, where):
        pltpu.make_async_remote_copy(
            src_ref=src,
            dst_ref=dst,
            send_sem=send_sem,
            recv_sem=recv_sem,
            device_id=where,
            device_id_type=MESH,
        ).start()

    def wait(ref, sem):
        pltpu.make_async_copy(ref, ref, sem).wait()

    up, down = lax.rem(z + 1, NZ), lax.rem(z + NZ - 1, NZ)
    other = dev(x, y, z, 1 - c)
    zdevs = [dev(x, y, lax.rem(z + d, NZ), c) for d in range(1, NZ)]
    ydevs = [dev(x, lax.rem(y + d, NY), z, c) for d in range(1, NY)]

    barrier = pltpu.get_barrier_semaphore()
    partners = zdevs + ydevs + [dev(lax.rem(x + 1, NX), y, z, c), dev(lax.rem(x + 3, NX), y, z, c), other]
    for p in partners:
        pl.semaphore_signal(barrier, inc=1, device_id=p, device_id_type=MESH)

    sub = lax.broadcasted_iota(jnp.int32, (ROWS, BR), 0)
    live0 = jnp.where(sub < length_ref[0], 1.0, 0.0).astype(F32)
    for m in range(NBLK):
        src_gd[m, 0] = start_ref[:, m * BR : (m + 1) * BR] * live0
        src_gd[m, 1] = diag_ref[:, m * BR : (m + 1) * BR]
    left_tile[...] = jnp.zeros((ROWS, BR), F32)
    for t in range(TPD):
        left_tile[:, t * ROWS : (t + 1) * ROWS] = left_ref[t]
    left_tile[:, TPD * ROWS : TPD * ROWS + 1] = jnp.full((ROWS, 1), length_ref[0].astype(F32), F32)
    shift_tile[...] = jnp.where(sub == 0, shift_ref[0], jnp.where(sub == 1, shift_ref[1], shift_ref[2]))

    pl.semaphore_wait(barrier, len(partners))

    p1 = (1 - c) * x + c * y
    p2 = (1 - c) * y + c * x

    def axis1(d):
        return dev(lax.rem(x + d * (1 - c) + 4, 4), lax.rem(y + d * c + 4, 4), z, c)

    def axis2(d):
        return dev(lax.rem(x + d * c + 4, 4), lax.rem(y + d * (1 - c) + 4, 4), z, c)

    def slot(d1, d2):
        q1, q2 = lax.rem(p1 + d1 + 4, 4), lax.rem(p2 + d2 + 4, 4)
        return (1 - c) * (q1 * 4 + q2) + c * (q2 * 4 + q1)

    H = BR // 2

    def part(d1, d2, half):
        s = slot(d1, d2)
        if half is None:
            return rbuf.at[s]
        return rbuf.at[s, :, pl.ds(half * H, H), :]

    def send_axis1():
        own = slot(0, 0)
        send(right_ref, rbuf.at[own], w_send, w_recv.at[0], axis1(1))
        send(right_ref, rbuf.at[own], w_send, w_recv.at[1], axis1(-1))

    def send_axis2(d1):
        src = right_ref if d1 == 0 else part(d1, 0, None)
        i = d1 % 4
        s = slot(d1, 0)
        send(src, rbuf.at[s], w_send, w_recv.at[4 + 4 * i], axis2(1))
        send(src, rbuf.at[s], w_send, w_recv.at[5 + 4 * i], axis2(-1))

    def first_of_axis1():
        wait(part(-1, 0, None), w_recv.at[0])
        send(part(-1, 0, 0), part(-1, 0, 0), w_send, w_recv.at[2], axis1(1))
        send_axis2(-1)

    def second_of_axis1():
        wait(part(1, 0, None), w_recv.at[1])
        send(part(1, 0, 1), part(1, 0, 1), w_send, w_recv.at[3], axis1(-1))
        send_axis2(1)

    def third_of_axis1():
        wait(part(2, 0, 0), w_recv.at[2])
        wait(part(2, 0, 1), w_recv.at[3])
        send_axis2(2)

    def near_axis2(d1):
        i = d1 % 4
        wait(part(d1, -1, None), w_recv.at[4 + 4 * i])
        send(part(d1, -1, 0), part(d1, -1, 0), w_send, w_recv.at[6 + 4 * i], axis2(1))
        wait(part(d1, 1, None), w_recv.at[5 + 4 * i])
        send(part(d1, 1, 1), part(d1, 1, 1), w_send, w_recv.at[7 + 4 * i], axis2(-1))

    def far_axis2(d1):
        i = d1 % 4
        wait(part(d1, 2, 0), w_recv.at[6 + 4 * i])
        wait(part(d1, 2, 1), w_recv.at[7 + 4 * i])

    send_axis1()
    send_axis2(0)

    src_line = lax.rem(z, 4)
    is_src = src_line == y
    kown = lax.div(z, 4)
    for p in ydevs:
        send(shift_tile, shift_all.at[y], st_send.at[0], st_recv.at[0], p)
    shift_all[y] = shift_tile[...]

    def blocks_of(zz):
        return pl.ds(4 * zz + 2 * c, 2)

    @pl.when(is_src)
    def _():
        for d in range(1, NZ):
            zt = lax.rem(z + d, NZ)
            send(src_gd.at[blocks_of(zt)], got_gd.at[kown], st_send.at[1], st_recv.at[1], dev(x, y, zt, c))
        got_gd[kown] = src_gd[blocks_of(z)]
        left_row[y] = left_tile[...]
        wait(got_gd.at[pl.ds(0, 3)], st_recv.at[1])

    @pl.when(jnp.logical_not(is_src))
    def _():
        send(left_tile, left_row.at[y], st_send.at[2], st_recv.at[2], dev(x, src_line, z, c))
        wait(got_gd, st_recv.at[1])

    G, D, GD, HV, Q, HD, U, K, UD = range(9)
    mine = blocks_of(z)
    for b in range(2):
        for k in range(KS):
            g = got_gd[k, b, 0]
            d = got_gd[k, b, 1]
            gd = g / d
            piece[G, k, b] = g
            piece[D, k, b] = d
            piece[GD, k, b] = gd
    v1[pl.ds(0, 4), mine] = piece[G]
    v1[pl.ds(4, 4), mine] = piece[GD]

    def ring(phase, v, width):
        def at(ch, zz):
            return v.at[pl.ds(ch * width, width), blocks_of(zz)]

        def start():
            for ch in range(2):
                send(at(ch, z), at(ch, z), ag_send.at[phase], ag_plus.at[phase, ch, 0], dev(x, y, up, c))
                send(at(ch, z), at(ch, z), ag_send.at[phase], ag_minus.at[phase, ch, 0], dev(x, y, down, c))
            for ch in range(2):
                send(at(ch, z), at(ch, z), ag_send.at[phase], ag_core.at[phase], other)

        def step(i):
            zp, zm = lax.rem(z + NZ - i, NZ), lax.rem(z + i, NZ)
            for ch in range(2):
                wait(at(ch, zp), ag_plus.at[phase, ch, i - 1])
                if i < 8:
                    send(at(ch, zp), at(ch, zp), ag_send.at[phase], ag_plus.at[phase, ch, i], dev(x, y, up, c))
                send(at(ch, zp), at(ch, zp), ag_send.at[phase], ag_core.at[phase], other)
                if i < 8:
                    wait(at(ch, zm), ag_minus.at[phase, ch, i - 1])
                    if i < 7:
                        send(at(ch, zm), at(ch, zm), ag_send.at[phase], ag_minus.at[phase, ch, i], dev(x, y, down, c))
                    send(at(ch, zm), at(ch, zm), ag_send.at[phase], ag_core.at[phase], other)

        def finish():
            wait(v.at[:, pl.ds(0, 32)], ag_core.at[phase])

        def sent():
            wait(v.at[:, pl.ds(0, 62)], ag_send.at[phase])

        return start, step, finish, sent

    start, step, finish, sent1 = ring(0, v1, 4)
    start()

    @pl.when(is_src)
    def _():
        wait(left_row.at[pl.ds(0, 3)], st_recv.at[2])
        for d in range(1, NZ):
            send(left_row, left_all.at[kown], st_send.at[2], st_recv.at[3], dev(x, y, lax.rem(z + d, NZ), c))
        left_all[kown] = left_row[...]

    first_of_axis1()
    step(1)
    second_of_axis1()
    near_axis2(0)
    step(2)
    third_of_axis1()
    step(3)
    near_axis2(-1)
    step(4)
    near_axis2(1)
    step(5)
    far_axis2(0)
    step(6)
    near_axis2(2)
    step(7)
    far_axis2(-1)
    far_axis2(1)
    step(8)

    wait(shift_all.at[pl.ds(0, 3)], st_recv.at[0])
    to_sm = pltpu.make_async_copy(shift_all, shift_sm, sm_sem)
    to_sm.start()

    @pl.when(is_src)
    def _():
        wait(left_all.at[pl.ds(0, 3)], st_recv.at[3])

    @pl.when(jnp.logical_not(is_src))
    def _():
        wait(left_all, st_recv.at[3])

    def widen(i, carry):
        k, yy = lax.div(i, 4), lax.rem(i, 4)
        tile = left_all[k, yy]
        for t in range(TPD):
            for j in range(ROWS):
                lane = t * ROWS + j
                left_wide[yy * TPD + t, k, j] = jnp.broadcast_to(tile[:, lane : lane + 1], (ROWS, BR))
        return carry

    lax.fori_loop(0, 16, widen, 0)
    subf = sub.astype(F32)
    for k in range(KS):
        length = jnp.broadcast_to(left_all[k, 0][:, TPD * ROWS : TPD * ROWS + 1], (ROWS, BR))
        mask[k] = jnp.where(subf < length, 1.0, 0.0).astype(F32)

    rbuf[slot(0, 0)] = right_ref[...]
    far_axis2(2)

    def cut(i, carry):
        for t in range(TPD):
            r = rbuf[i, t]
            hi = r.astype(BF16)
            r_hi[i, t] = hi
            r_lo[i, t] = (r - hi.astype(F32)).astype(BF16)
        return carry

    lax.fori_loop(0, 16, cut, 0)
    to_sm.wait()
    finish()

    def product(v, nk):
        rows = nk * ROWS
        y_own[:, pl.ds(0, nk)] = jnp.zeros((4, nk, ROWS, BR), F32)

        def body(i, carry):
            yy, t = lax.div(i, TPD), lax.rem(i, TPD)
            shift = shift_sm[yy, t, 0]
            for n in range(4):
                m = 4 * z + n + shift
                m = jnp.where(m >= NBLK, m - NBLK, m)
                tiles = []
                for k in range(nk):
                    src = v[k, m]
                    total = None
                    for j in range(ROWS):
                        term = left_wide[i, k % KS, j] * src[j : j + 1, :]
                        total = term if total is None else total + term
                    tiles.append(total)
                p = jnp.concatenate(tiles, axis=0)
                hi = p.astype(BF16)
                lo = (p - hi.astype(F32)).astype(BF16)
                rh = r_hi[n * 4 + yy, t]
                rl = r_lo[n * 4 + yy, t]
                both = jnp.dot(jnp.concatenate([hi, lo], axis=0), rh, preferred_element_type=F32)
                more = jnp.dot(hi, rl, preferred_element_type=F32)
                res = both[:rows] + both[rows:] + more
                y_own[n, pl.ds(0, nk)] += res.reshape(nk, ROWS, BR)
            return carry

        lax.fori_loop(0, 4 * TPD, body, 0)

    def swap(phase, y_in, nk):
        send(
            y_own.at[pl.ds(2 * (1 - c), 2), pl.ds(0, nk)], y_in, y_send.at[phase], y_recv.at[phase], other
        )
        wait(y_in, y_recv.at[phase])

    def swapped(phase, y_in):
        wait(y_in, y_send.at[phase])

    product(v1, 8)
    swap(0, y_in1, 8)
    for b in range(2):
        for k in range(KS):
            h = (y_own[2 * c + b, k] + y_in1[b, k]) * mask[k]
            q = (y_own[2 * c + b, KS + k] + y_in1[b, KS + k]) * mask[k]
            piece[HV, k, b] = h
            piece[Q, k, b] = q
            piece[HD, k, b] = h / piece[D, k, b]
    v2[:, mine] = piece[HD]
    start, step, finish, sent2 = ring(1, v2, 2)
    start()

    def dot(a, b):
        prod = (piece[a] * piece[b]).reshape(KS * 2, ROWS, BR)
        return jnp.sum(jnp.sum(prod, axis=0), axis=0, keepdims=True)

    def dots_z(g, pairs):
        for r, (a, b) in enumerate(pairs):
            dz[g, z, r : r + 1, :] = dot(a, b)
        for p in zdevs:
            send(dz.at[g, z], dz.at[g, z], dot_send.at[g, 0], dot_recv.at[g, 0], p)

    def dots_plane(g):
        wait(dz.at[g, pl.ds(0, 15)], dot_recv.at[g, 0])
        here = x * 4 + y
        dp[g, here] = jnp.sum(dz[g], axis=0)
        for d in range(1, 16):
            there = dev(lax.rem(x + d // 4, 4), lax.rem(y + d % 4, 4), z, c)
            send(dp.at[g, here], dp.at[g, here], dot_send.at[g, 1], dot_recv.at[g, 1], there)

    def dots_core(g):
        wait(dp.at[g, pl.ds(0, 15)], dot_recv.at[g, 1])
        dc[g, c] = jnp.sum(dp[g], axis=0)
        send(dc.at[g, c], dc.at[g, c], dot_send.at[g, 2], dot_recv.at[g, 2], other)

    def dots_done(g, count):
        wait(dc.at[g, 1 - c], dot_recv.at[g, 2])
        total = jnp.sum(dc[g, 0] + dc[g, 1], axis=1, keepdims=True)
        return [jnp.broadcast_to(total[r : r + 1, :], (ROWS, BR)) for r in range(count)]

    def dots_sent(g):
        wait(dz.at[g, pl.ds(0, 15)], dot_send.at[g, 0])
        wait(dp.at[g, pl.ds(0, 15)], dot_send.at[g, 1])
        wait(dc.at[g, c], dot_send.at[g, 2])

    for g in range(3):
        dz[g, z] = jnp.zeros((16, BR), F32)
    dots_z(0, [(G, G), (G, HV), (G, HD), (G, GD)])
    step(1)
    step(2)
    step(3)
    dots_plane(0)
    step(4)
    step(5)
    dots_core(0)
    step(6)
    step(7)
    step(8)
    gg, gh, ghd, ggd = dots_done(0, 4)
    f1 = jnp.sqrt(CELLS / (gg + EPS))
    r1 = f1 * f1 * gh / CELLS
    c1 = f1 * f1 * (ghd - r1 * ggd) / CELLS
    finish()
    swapped(0, y_in1)

    product(v2, 4)
    swap(1, y_in2, 4)
    for b in range(2):
        for k in range(KS):
            w = (y_own[2 * c + b, k] + y_in2[b, k]) * mask[k]
            u = f1 * (piece[HD, k, b] - r1 * piece[GD, k, b] - c1 * piece[G, k, b])
            piece[U, k, b] = u
            piece[UD, k, b] = u / piece[D, k, b]
            piece[K, k, b] = f1 * (w - r1 * piece[Q, k, b] - c1 * piece[HV, k, b])
    dots_z(
        1,
        [(U, U), (G, K), (U, HV), (U, K), (GD, K), (G, UD), (U, HD), (UD, K), (U, UD)],
    )
    dots_plane(1)
    dots_core(1)
    uu, gk, uh, uk, gkd, gud, uhd, ukd, uud = dots_done(1, 9)
    f2 = jnp.sqrt(CELLS / (uu + EPS))
    a = r1
    b_ = f1 * f2 * (gk + uh) / (2.0 * CELLS)
    d_ = f2 * f2 * uk / CELLS
    h_ = (a - d_) / 2.0
    ritz = (a + d_) / 2.0 - jnp.sqrt(h_ * h_ + b_ * b_)
    big = jnp.maximum(jnp.abs(h_), jnp.abs(b_))
    safe = jnp.where(big > 0.0, big, 1.0)
    hs = jnp.where(big > 0.0, h_ / safe, 1.0)
    bs = b_ / safe
    rs = jnp.sqrt(hs * hs + bs * bs)
    larger = jnp.sqrt((rs + jnp.abs(hs)) / (2.0 * rs))
    smaller = jnp.abs(bs) / (2.0 * rs * larger)
    sign = jnp.where(bs < 0.0, -1.0, 1.0)
    co = jnp.where(hs >= 0.0, larger, smaller)
    si = sign * jnp.where(hs >= 0.0, smaller, larger)
    n1, n2 = -si * f1, co * f2
    e1 = f1 * (n1 * (ghd - ritz * ggd) + n2 * (gkd - ritz * gud)) / CELLS
    e2 = f2 * (n1 * (uhd - ritz * gud) + n2 * (ukd - ritz * uud)) / CELLS
    for b in range(2):
        for k in range(KS):
            g = piece[G, k, b]
            u = piece[U, k, b]
            t2 = (n1 * (piece[HV, k, b] - ritz * g) + n2 * (piece[K, k, b] - ritz * u)) / piece[D, k, b]
            piece[Q, k, b] = t2 - e1 * f1 * g - e2 * f2 * u
    v3[:, mine] = piece[Q]
    start, step, finish, sent3 = ring(2, v3, 2)
    start()
    dots_z(2, [(Q, Q)])
    step(1)
    step(2)
    step(3)
    dots_plane(2)
    step(4)
    step(5)
    dots_core(2)
    step(6)
    step(7)
    step(8)
    (qq,) = dots_done(2, 1)
    f3 = jnp.sqrt(CELLS / (qq + EPS))
    finish()
    swapped(1, y_in2)

    product(v3, 4)
    swap(2, y_in3, 4)
    for b in range(2):
        for k in range(KS):
            out_src[k, 0, b] = piece[Q, k, b] * f3
            out_src[k, 1, b] = (y_own[2 * c + b, k] + y_in3[b, k]) * mask[k] * f3

    yo, co_ = lax.div(z, 4), lax.rem(lax.div(z, 2), 2)
    part_out = lax.rem(z, 2) * 2 + c
    stays = jnp.logical_and(jnp.logical_and(yo == y, src_line == y), co_ == c)
    for k in range(KS):
        here = jnp.logical_and(stays, kown == k)

        @pl.when(here)
        def _():
            out_got[part_out] = out_src[k]

        @pl.when(jnp.logical_not(here))
        def _():
            send(out_src.at[k], out_got.at[part_out], out_send, out_recv, dev(x, yo, y + 4 * k, co_))

    @pl.when(stays)
    def _():
        wait(out_got.at[pl.ds(0, 3)], out_recv)
        wait(out_got.at[pl.ds(0, 3)], out_send)

    @pl.when(jnp.logical_not(stays))
    def _():
        wait(out_got, out_recv)
        wait(out_got, out_send)

    for s in range(4):
        for b in range(2):
            col = (s * 2 + b) * BR
            basis_ref[:, col : col + BR] = out_got[s, 0, b]
            image_ref[:, col : col + BR] = out_got[s, 1, b]

    wait(rbuf.at[pl.ds(0, 15)], w_send)
    sent1()
    sent2()
    sent3()
    swapped(2, y_in3)
    for g in range(3):
        dots_sent(g)
    wait(shift_all.at[pl.ds(0, 3)], st_send.at[0])

    @pl.when(is_src)
    def _():
        wait(src_gd.at[pl.ds(0, 30)], st_send.at[1])
        wait(src_gd.at[pl.ds(0, 30)], st_send.at[2])

    @pl.when(jnp.logical_not(is_src))
    def _():
        wait(left_tile, st_send.at[2])


def per_device(start_vector, precond_diag, left_env, right_env, right_shift, sector_length):
    vmem = pl.BlockSpec(memory_space=pltpu.VMEM)
    smem = pl.BlockSpec(memory_space=pltpu.SMEM)
    DMA = pltpu.SemaphoreType.DMA
    tile = (ROWS, BR)
    return pl.pallas_call(
        kernel,
        out_shape=[jax.ShapeDtypeStruct((ROWS, 1024), F32)] * 2,
        in_specs=[vmem, vmem, vmem, vmem, smem, smem],
        out_specs=[vmem, vmem],
        scratch_shapes=[
            pltpu.VMEM((16, TPD, BR, BR), F32),
            pltpu.VMEM((16, TPD, BR, BR), BF16),
            pltpu.VMEM((16, TPD, BR, BR), BF16),
            pltpu.VMEM((8, NBLK) + tile, F32),
            pltpu.VMEM((4, NBLK) + tile, F32),
            pltpu.VMEM((4, NBLK) + tile, F32),
            pltpu.VMEM((4, 8) + tile, F32),
            pltpu.VMEM((2, 8) + tile, F32),
            pltpu.VMEM((2, 4) + tile, F32),
            pltpu.VMEM((2, 4) + tile, F32),
            pltpu.VMEM((9, KS, 2) + tile, F32),
            pltpu.VMEM((NBLK, 2) + tile, F32),
            pltpu.VMEM((KS, 2, 2) + tile, F32),
            pltpu.VMEM(tile, F32),
            pltpu.VMEM((4,) + tile, F32),
            pltpu.VMEM((KS, 4) + tile, F32),
            pltpu.VMEM(tile, jnp.int32),
            pltpu.VMEM((4,) + tile, jnp.int32),
            pltpu.SMEM((4,) + tile, jnp.int32),
            pltpu.VMEM((4 * TPD, KS, ROWS) + tile, F32),
            pltpu.VMEM((KS,) + tile, F32),
            pltpu.VMEM((3, 16, 16, BR), F32),
            pltpu.VMEM((3, 16, 16, BR), F32),
            pltpu.VMEM((3, 2, 16, BR), F32),
            pltpu.VMEM((KS, 2, 2) + tile, F32),
            pltpu.VMEM((4, 2, 2) + tile, F32),
            DMA,
            DMA((20,)),
            DMA((3,)),
            DMA((3, 2, 8)),
            DMA((3, 2, 7)),
            DMA((3,)),
            DMA((3,)),
            DMA((3,)),
            DMA((3, 3)),
            DMA((3, 3)),
            DMA((3,)),
            DMA((4,)),
            DMA,
            DMA,
            DMA,
        ],
        compiler_params=pltpu.CompilerParams(
            collective_id=0, has_side_effects=True, vmem_limit_bytes=48 * 1024 * 1024
        ),
        cost_estimate=pl.CostEstimate(flops=600_000_000, bytes_accessed=2_000_000, transcendentals=0),
    )(start_vector, precond_diag, left_env, right_env, right_shift, sector_length)


def solution(mesh):
    placed = (
        P("sec", None),
        P("sec", None),
        P("mpo", "sec", None),
        P("mpo", "sec", None),
        P("mpo"),
        P("sec"),
    )
    return jax.shard_map(
        per_device,
        mesh=mesh,
        in_specs=placed,
        out_specs=(P("sec", "mpo"), P("sec", "mpo")),
        check_vma=False,
    )
```

time: 1320 us -> 152 us (0.12)
  the two profiles are of different devices: /device:TPU:1 before, /device:TPU:16 now
where the time goes in v1:
time: 152 us
  Pallas kernels  146 us (96%)
  local copies, waits for them, and re-layouts  4.76 us (3%)
    pallas_call x1, Pallas kernels, per_device(): pl.pallas_call(kernel, out_shape=[jax.ShapeDtypeStruct((ROWS, 1024), F32)...  146 us
    unnamed x12, local copies, waits for them, and re-layouts  4.76 us

profile of v1, /device:TPU:16, one launch (start us, length us, event | category | flops | bytes accessed | tf_op | source)
XLA Modules:
  0.0 152.0 jit_solution(9407789298626677163)
XLA Ops:
  0.6 0.0 copy-start.4
  1.3 0.0 copy-done.4
  1.3 0.0 copy-start
  1.3 0.9 copy-done
  2.3 0.0 copy-start.1
  2.3 0.9 copy-done.1
  3.2 0.0 copy-start.2
  3.2 0.9 copy-done.2
  4.1 0.0 copy-start.3
  4.1 0.7 copy-done.3
  4.8 145.9 %shard_map.77 = (f32[8,1024]{1,0:T(8,128)S(1)}, f32[8,1024]{1,0:T(8,128)S(1)}) custom-call(f32[8,8192]{1,0:T(8,128)S(1)} %copy-done, f32[8,8192]{1,0:T(8,128)S(1)} %copy-done.1, f32[3,8,8]{2,1,0:T(8,128)S(1)} %copy-done.3, f32[3,128,128]{2,1,0:T(8,128)S(1)} %copy-done.2, s32[3]{0:T(128)S(1)} %copy-done.4, s32[1]{0:T(128)S(6)} %copy.10.length_ref), custom_call_target="tpu_custom_call" | custom-call | flops 600000000 | bytes 2000000 | tf_op jit(solution)/shard_map/pallas_call | solution.py:547
  150.8 0.6 copy.11
  151.4 0.6 copy.12
Async XLA Ops:
  0.6 0.7 copy-start.4
  1.3 1.0 copy-start
  2.3 0.9 copy-start.1
  3.2 0.9 copy-start.2
  4.1 0.7 copy-start.3

commit v2 on v0

v2 whole, which is shorter than its diff:
```python
import jax
import jax.numpy as jnp
from jax import lax
from jax.experimental import pallas as pl
from jax.experimental.pallas import tpu as pltpu
from jax.sharding import PartitionSpec as P

MESH = pl.DeviceIdType.MESH
F32 = jnp.float32
BF16 = jnp.bfloat16

NZ = 16
ROWS, BR, NBLK = 8, 128, 64
TPD = 3
TERMS = 24
KS = 4
CELLS = float(512 * 8192)
EPS = 1e-6
TILE = (ROWS, BR)

G, B, E, H_, Q, S, A_, AA, AQ, P_, T, W, AP = range(13)
EARLY = [
    (G, G), (G, B), (G, A_), (B, B), (A_, B), (A_, A_), (G, H_), (G, Q), (B, Q), (A_, H_), (A_, Q),
    (E, B), (E, A_), (AA, A_), (E, Q), (AA, Q), (E, E), (E, AA), (AA, AA), (E, AQ), (AA, AQ), (AQ, AQ),
]
LATE = [(G, P_), (B, P_), (A_, P_), (E, P_), (AA, P_), (E, AP), (AA, AP), (AQ, AP), (AP, AP)]


def kernel(
    start_hbm,
    diag_hbm,
    left_ref,
    right_hbm,
    shift_ref,
    length_ref,
    basis_ref,
    image_ref,
    start_ref,
    diag_ref,
    zbuf,
    rbuf,
    r_hi,
    r_lo,
    gd,
    v1,
    v2,
    v2b,
    v3,
    y_sum,
    piece,
    inv,
    left_all,
    shift_all,
    shift_sm,
    left_wide,
    mask,
    dz0,
    dp0,
    dc0,
    dz1,
    dp1,
    dc1,
    out_src,
    out_got,
    in_sem,
    z_send,
    z_plus,
    z_minus,
    r_send,
    r_recv,
    x_send,
    x_recv,
    x_core,
    l_send,
    l_recv,
    s_send,
    s_recv,
    sm_sem,
    ag_send,
    ag_recv,
    ag_core,
    dot_send,
    dot_recv,
    out_send,
    out_recv,
):
    sec = lax.axis_index("sec")
    mpo = lax.axis_index("mpo")
    z, x = lax.div(sec, 4), lax.rem(sec, 4)
    y, c = lax.div(mpo, 2), lax.rem(mpo, 2)
    here = 4 * y + x

    def dev(xx, yy, zz, cc):
        return (zz * 4 + xx, yy * 2 + cc)

    def send(src, dst, send_sem, recv_sem, where):
        pltpu.make_async_remote_copy(
            src_ref=src,
            dst_ref=dst,
            send_sem=send_sem,
            recv_sem=recv_sem,
            device_id=where,
            device_id_type=MESH,
        ).start()

    def wait(ref, sem):
        pltpu.make_async_copy(ref, ref, sem).wait()

    up = dev(x, y, lax.rem(z + 1, NZ), c)
    down = dev(x, y, lax.rem(z + NZ - 1, NZ), c)
    other = dev(x, y, z, 1 - c)
    zdevs = [dev(x, y, lax.rem(z + d, NZ), c) for d in range(1, NZ)]
    offsets = sorted(range(1, 16), key=lambda o: -(min(o // 4, 4 - o // 4) + min(o % 4, 4 - o % 4)))

    def peer(o):
        return dev(lax.rem(x + o // 4, 4), lax.rem(y + o % 4, 4), z, c)

    def sender(o):
        return 4 * lax.rem(y + 4 - o % 4, 4) + lax.rem(x + 4 - o // 4, 4)

    loads = [
        pltpu.make_async_copy(right_hbm, zbuf.at[z], in_sem.at[0]),
        pltpu.make_async_copy(start_hbm, start_ref, in_sem.at[1]),
        pltpu.make_async_copy(diag_hbm, diag_ref, in_sem.at[2]),
    ]
    for load in loads:
        load.start()
    barrier = pltpu.get_barrier_semaphore()
    partners = [up, down, other] + [peer(o) for o in offsets]
    partners += [dev(x, lax.rem(y + d, 4), z, 1 - c) for d in range(1, 4)]
    for p in partners:
        pl.semaphore_signal(barrier, inc=1, device_id=p, device_id_type=MESH)

    sub = lax.broadcasted_iota(jnp.int32, TILE, 0)
    left_all[c, here] = jnp.zeros(TILE, F32)
    for t in range(TPD):
        left_all[c, here, :, t * ROWS : (t + 1) * ROWS] = left_ref[t]
    left_all[c, here, :, TPD * ROWS : TPD * ROWS + 1] = jnp.full((ROWS, 1), length_ref[0].astype(F32), F32)
    shift_all[c, y] = jnp.where(sub == 0, shift_ref[0], jnp.where(sub == 1, shift_ref[1], shift_ref[2]))
    live0 = jnp.where(sub < length_ref[0], 1.0, 0.0).astype(F32)
    loads[1].wait()
    loads[2].wait()
    for m in range(NBLK):
        gd[x, m % 16, m // 16, 0] = start_ref[:, m * BR : (m + 1) * BR] * live0
        gd[x, m % 16, m // 16, 1] = diag_ref[:, m * BR : (m + 1) * BR]
    loads[0].wait()
    pl.semaphore_wait(barrier, len(partners))

    def deliver(zz, t):
        nn = lax.rem(lax.div(zz, 4), 2)
        yd, cd = lax.rem(zz, 4), lax.div(zz, 8)
        dst = rbuf.at[nn, y, c, t]
        stays = jnp.logical_and(yd == y, cd == c)

        @pl.when(stays)
        def _():
            pltpu.make_async_copy(zbuf.at[zz, t], dst, r_recv).start()

        @pl.when(jnp.logical_not(stays))
        def _():
            send(zbuf.at[zz, t], dst, r_send, r_recv, dev(x, yd, z, cd))

    for t in range(TPD):
        send(zbuf.at[z, t], zbuf.at[z, t], z_send, z_plus.at[t, 0], up)
        send(zbuf.at[z, t], zbuf.at[z, t], z_send, z_minus.at[t, 0], down)

    def half(k, cc):
        return gd.at[k, :, pl.ds(2 * cc, 2)]

    for d in (2, 1, 3):
        send(half(x, c), half(x, c), x_send, x_recv.at[d - 1], dev(lax.rem(x + d, 4), y, z, c))
    for d in range(1, 4):
        send(shift_all.at[c, y], shift_all.at[c, y], s_send.at[0], s_recv.at[0], dev(x, lax.rem(y + d, 4), z, c))
    for o in offsets:
        send(left_all.at[c, here], left_all.at[c, here], l_send.at[0], l_recv.at[0], peer(o))
    for t in range(TPD):
        deliver(z, t)

    def ring_step(i, t):
        zp, zm = lax.rem(z + NZ - i, NZ), lax.rem(z + i, NZ)
        wait(zbuf.at[zp, t], z_plus.at[t, i - 1])
        if i < 8:
            send(zbuf.at[zp, t], zbuf.at[zp, t], z_send, z_plus.at[t, i], up)
        deliver(zp, t)
        if i < 8:
            wait(zbuf.at[zm, t], z_minus.at[t, i - 1])
            if i < 7:
                send(zbuf.at[zm, t], zbuf.at[zm, t], z_send, z_minus.at[t, i], down)
            deliver(zm, t)

    def pass_rows(d):
        k = lax.rem(x + 4 - d, 4)
        wait(half(k, c), x_recv.at[d - 1])
        send(half(k, c), half(k, c), x_send, x_core, other)

    def pass_small():
        wait(shift_all.at[c, pl.ds(0, 3)], s_recv.at[0])
        send(shift_all.at[c], shift_all.at[c], s_send.at[1], s_recv.at[1], other)
        wait(left_all.at[c, pl.ds(0, 15)], l_recv.at[0])
        send(left_all.at[c], left_all.at[c], l_send.at[1], l_recv.at[1], other)

    to_sm = pltpu.make_async_copy(shift_all, shift_sm, sm_sem)

    def take_small():
        wait(shift_all.at[1 - c], s_recv.at[1])
        to_sm.start()
        wait(left_all.at[1 - c], l_recv.at[1])
        for k in range(KS):
            length = jnp.broadcast_to(left_all[c, 4 * y + k][:, TPD * ROWS : TPD * ROWS + 1], TILE)
            mask[k] = jnp.where(sub.astype(F32) < length, 1.0, 0.0).astype(F32)

    def widen(first, count):
        def body(i, carry):
            cc, r = lax.div(i, 16), lax.rem(i, 16)
            yy, k = lax.div(r, 4), lax.rem(r, 4)
            tile = left_all[cc, r]
            for t in range(TPD):
                for j in range(ROWS):
                    lane = t * ROWS + j
                    left_wide[(yy * 2 + cc) * TPD + t, k, j] = jnp.broadcast_to(tile[:, lane : lane + 1], TILE)
            return carry

        lax.fori_loop(first, first + count, body, 0)

    def take_rows():
        wait(gd.at[pl.ds(0, 3), :, pl.ds(0, 2)], x_core)

    def vectors(first, count):
        def body(r, carry):
            for k in range(KS):
                for j in range(4):
                    g = gd[k, r, j, 0]
                    a = 1.0 / gd[k, r, j, 1]
                    b = g * a
                    v1[k, r, j] = g
                    v1[KS + k, r, j] = b
                    v1[2 * KS + k, r, j] = b * a
            return carry

        lax.fori_loop(first, first + count, body, 0)

    idle = [lambda: None]
    tasks = idle * 3 + [pass_small] + idle + [take_small]
    tasks += [lambda i=i: widen(4 * i, 4) for i in range(8)]
    tasks += [lambda: pass_rows(1), lambda: pass_rows(3), lambda: pass_rows(2), take_rows]
    tasks += [lambda i=i: vectors(3 * i, 3) for i in range(5)] + [lambda: vectors(15, 1)]
    tasks = tasks[::-1]
    for i in range(1, 9):
        for t in range(TPD):
            ring_step(i, t)
            if tasks:
                tasks.pop()()
    while tasks:
        tasks.pop()()

    for nn in range(2):
        for k in range(KS):
            j = 2 * c + nn
            inv[k, nn] = 1.0 / gd[k, here, j, 1]
            piece[G, k, nn] = v1[k, here, j]
            piece[B, k, nn] = v1[KS + k, here, j]
            piece[E, k, nn] = v1[2 * KS + k, here, j]
    to_sm.wait()
    wait(rbuf, r_recv)

    def product(v, nk, cut):
        rows = nk * ROWS
        y_sum[:, pl.ds(0, nk)] = jnp.zeros((2, nk) + TILE, F32)

        def body(i, carry):
            yy, rest = lax.div(i, 2 * TPD), lax.rem(i, 2 * TPD)
            cc, t = lax.div(rest, TPD), lax.rem(rest, TPD)
            shift = shift_sm[cc, yy, t, 0]
            for nn in range(2):
                m = 16 * (2 * c + nn) + here + shift
                m = jnp.where(m >= NBLK, m - NBLK, m)
                r, j4 = lax.rem(m, 16), lax.div(m, 16)
                tiles = []
                for k in range(nk):
                    src = v[k, r, j4]
                    total = None
                    for j in range(ROWS):
                        term = left_wide[i, k % KS, j] * src[j : j + 1, :]
                        total = term if total is None else total + term
                    tiles.append(total)
                p = jnp.concatenate(tiles, axis=0)
                hi = p.astype(BF16)
                lo = (p - hi.astype(F32)).astype(BF16)
                if cut:
                    full = rbuf[nn, yy, cc, t]
                    rh = full.astype(BF16)
                    rl = (full - rh.astype(F32)).astype(BF16)
                    r_hi[nn, yy, cc, t] = rh
                    r_lo[nn, yy, cc, t] = rl
                else:
                    rh = r_hi[nn, yy, cc, t]
                    rl = r_lo[nn, yy, cc, t]
                both = jnp.dot(jnp.concatenate([hi, lo], axis=0), rh, preferred_element_type=F32)
                more = jnp.dot(hi, rl, preferred_element_type=F32)
                y_sum[nn, pl.ds(0, nk)] += (both[:rows] + both[rows:] + more).reshape((nk,) + TILE)
            return carry

        lax.fori_loop(0, TERMS, body, 0)

    def gather(phase, v):
        def at(r, cc):
            return v.at[:, r, pl.ds(2 * cc, 2)]

        def start():
            for o in offsets:
                send(at(here, c), at(here, c), ag_send.at[phase, 0], ag_recv.at[phase, o], peer(o))
            send(at(here, c), at(here, c), ag_send.at[phase, 1], ag_core.at[phase], other)

        def pass_on():
            for o in offsets[::-1]:
                r = sender(o)
                wait(at(r, c), ag_recv.at[phase, o])
                send(at(r, c), at(r, c), ag_send.at[phase, 1], ag_core.at[phase], other)

        def finish():
            wait(v.at[:, :, pl.ds(0, 2)], ag_core.at[phase])

        def sent():
            wait(v.at[:, pl.ds(0, 15), pl.ds(0, 2)], ag_send.at[phase, 0])
            wait(v.at[:, :, pl.ds(0, 2)], ag_send.at[phase, 1])

        return start, pass_on, finish, sent

    def dots(g, dz, dp, dc):
        def start(pairs):
            dz[z] = jnp.zeros(dz.shape[1:], F32)
            for r, (a, b) in enumerate(pairs):
                prod = (piece[a] * piece[b]).reshape((2 * KS,) + TILE)
                dz[z, r : r + 1, :] = jnp.sum(jnp.sum(prod, axis=0), axis=0, keepdims=True)
            for p in zdevs:
                send(dz.at[z], dz.at[z], dot_send.at[g, 0], dot_recv.at[g, 0], p)

        def plane():
            wait(dz.at[pl.ds(0, 15)], dot_recv.at[g, 0])
            dp[here] = jnp.sum(dz[...], axis=0)
            for o in offsets:
                send(dp.at[here], dp.at[here], dot_send.at[g, 1], dot_recv.at[g, 1], peer(o))

        def core():
            wait(dp.at[pl.ds(0, 15)], dot_recv.at[g, 1])
            dc[c] = jnp.sum(dp[...], axis=0)
            send(dc.at[c], dc.at[c], dot_send.at[g, 2], dot_recv.at[g, 2], other)

        def done(pairs):
            wait(dc.at[1 - c], dot_recv.at[g, 2])
            total = jnp.sum(dc[0] + dc[1], axis=1, keepdims=True)
            return {p: jnp.broadcast_to(total[r : r + 1, :], TILE) for r, p in enumerate(pairs)}

        def sent():
            wait(dz.at[pl.ds(0, 15)], dot_send.at[g, 0])
            wait(dp.at[pl.ds(0, 15)], dot_send.at[g, 1])
            wait(dc.at[c], dot_send.at[g, 2])

        return start, plane, core, done, sent

    product(v1, 3 * KS, True)
    mine = pl.ds(2 * c, 2)
    for nn in range(2):
        for k in range(KS):
            h = y_sum[nn, k] * mask[k]
            q = y_sum[nn, KS + k] * mask[k]
            a = h * inv[k, nn]
            piece[H_, k, nn] = h
            piece[Q, k, nn] = q
            piece[S, k, nn] = y_sum[nn, 2 * KS + k] * mask[k]
            piece[A_, k, nn] = a
            piece[AA, k, nn] = a * inv[k, nn]
            piece[AQ, k, nn] = q * inv[k, nn]
    v2[:, here, mine] = piece[A_]
    v2b[pl.ds(0, KS), here, mine] = piece[AA]
    v2b[pl.ds(KS, KS), here, mine] = piece[AQ]
    ag2, ag2b, ag3 = gather(0, v2), gather(1, v2b), gather(2, v3)
    early, late = dots(0, dz0, dp0, dc0), dots(1, dz1, dp1, dc1)
    ag2[0]()
    early[0](EARLY)
    ag2b[0]()
    ag2[1]()
    ag2[2]()

    product(v2, KS, False)
    for nn in range(2):
        for k in range(KS):
            p = y_sum[nn, k] * mask[k]
            piece[P_, k, nn] = p
            piece[AP, k, nn] = p * inv[k, nn]
    v3[:, here, mine] = piece[AP]
    ag3[0]()
    late[0](LATE)
    early[1]()
    ag2b[1]()
    ag2b[2]()
    product(v2b, 2 * KS, False)
    for nn in range(2):
        for k in range(KS):
            piece[T, k, nn] = y_sum[nn, k] * mask[k]
            piece[W, k, nn] = y_sum[nn, KS + k] * mask[k]
    early[2]()
    ag3[1]()
    late[1]()
    ag3[2]()

    product(v3, KS, False)
    late[2]()
    dot = early[3](EARLY)
    dot.update(late[3](LATE))
    dot.update({(b, a): value for (a, b), value in dot.items()})

    f1 = jnp.sqrt(CELLS / (dot[G, G] + EPS))
    r1 = f1 * f1 * dot[G, H_] / CELLS
    c1 = f1 * f1 * (dot[G, A_] - r1 * dot[G, B]) / CELLS
    w = (-f1 * c1, -f1 * r1, f1)
    x_x = [[dot[i, j] for j in (G, B, A_)] for i in (G, B, A_)]
    x_y = [
        [dot[G, H_], dot[G, Q], dot[G, P_]],
        [dot[G, A_], dot[B, Q], dot[B, P_]],
        [dot[A_, H_], dot[A_, Q], dot[A_, P_]],
    ]
    ax_y = [
        [dot[G, A_], dot[B, Q], dot[B, P_]],
        [dot[A_, B], dot[E, Q], dot[E, P_]],
        [dot[A_, A_], dot[AA, Q], dot[AA, P_]],
    ]
    ax_x = [
        [dot[G, B], dot[B, B], dot[A_, B]],
        [dot[B, B], dot[E, B], dot[E, A_]],
        [dot[A_, B], dot[E, A_], dot[AA, A_]],
    ]

    def along(row):
        return w[0] * row[0] + w[1] * row[1] + w[2] * row[2]

    def form(m):
        return along([along(row) for row in m])

    def column(m, j):
        return [row[j] for row in m]

    uu, uk, uak, uau = form(x_x), form(x_y), form(ax_y), form(ax_x)
    gu, gk, uh = along(x_x[0]), along(x_y[0]), along(column(x_y, 0))
    gak, gau, uah = along(x_y[1]), along(x_x[1]), along(column(x_x, 2))
    f2 = jnp.sqrt(CELLS / (jnp.maximum(uu, 0.0) + EPS))
    b_ = f1 * f2 * (gk + uh) / (2.0 * CELLS)
    d_ = f2 * f2 * uk / CELLS
    h_ = (r1 - d_) / 2.0
    ritz = (r1 + d_) / 2.0 - jnp.sqrt(h_ * h_ + b_ * b_)
    big = jnp.maximum(jnp.abs(h_), jnp.abs(b_))
    safe = jnp.where(big > 0.0, big, 1.0)
    hs = jnp.where(big > 0.0, h_ / safe, 1.0)
    bs = b_ / safe
    rs = jnp.sqrt(hs * hs + bs * bs)
    larger = jnp.sqrt((rs + jnp.abs(hs)) / (2.0 * rs))
    smaller = jnp.abs(bs) / (2.0 * rs * larger)
    co = jnp.where(hs >= 0.0, larger, smaller)
    si = jnp.where(bs < 0.0, -1.0, 1.0) * jnp.where(hs >= 0.0, smaller, larger)
    n1, n2 = -si * f1, co * f2
    e1 = f1 * (n1 * (dot[G, A_] - ritz * dot[G, B]) + n2 * (gak - ritz * gau)) / CELLS
    e2 = f2 * (n1 * (uah - ritz * gau) + n2 * (uak - ritz * uau)) / CELLS
    t2 = {
        A_: n1 + n2 * w[0],
        B: -ritz * (n1 + n2 * w[0]),
        E: -ritz * n2 * w[1],
        AA: -ritz * n2 * w[2],
        AQ: n2 * w[1],
        AP: n2 * w[2],
    }
    dot[A_, AQ], dot[A_, AP], dot[B, AQ], dot[B, AP] = dot[AA, Q], dot[AA, P_], dot[E, Q], dot[E, P_]
    dot[B, AA] = dot[E, A_]
    dot.update({(b, a): value for (a, b), value in dot.items()})
    tt = jnp.zeros(TILE, F32)
    for i in t2:
        row = jnp.zeros(TILE, F32)
        for j in t2:
            row = row + t2[j] * dot[i, j]
        tt = tt + t2[i] * row
    square = tt - 2.0 * CELLS * (e1 * e1 + e2 * e2)
    square = square + e1 * e1 * f1 * f1 * dot[G, G] + e2 * e2 * f2 * f2 * uu + 2.0 * e1 * e2 * f1 * f2 * gu
    f3 = jnp.sqrt(CELLS / (jnp.maximum(square, 0.0) + EPS))
    coef = dict(t2)
    coef[G] = -e1 * f1 - e2 * f2 * w[0]
    coef[B] = coef[B] - e2 * f2 * w[1]
    coef[A_] = coef[A_] - e2 * f2 * w[2]
    coef = {i: f3 * value for i, value in coef.items()}
    image_of = {A_: P_, B: Q, E: S, AA: T, AQ: W, G: H_}
    for nn in range(2):
        for k in range(KS):
            basis = coef[AP] * piece[AP, k, nn]
            image = coef[AP] * (y_sum[nn, k] * mask[k])
            for i in image_of:
                basis = basis + coef[i] * piece[i, k, nn]
                image = image + coef[i] * piece[image_of[i], k, nn]
            out_src[k, nn, 0] = basis
            out_src[k, nn, 1] = image

    spot = 4 * lax.rem(y, 2) + x
    cd = lax.div(y, 2)
    keeps = cd == c
    for k in range(KS):
        for nn in range(2):
            stays = jnp.logical_and(jnp.logical_and(x == k, y == 2 * c + nn), keeps)

            @pl.when(stays)
            def _():
                out_got[spot] = out_src[k, nn]

            @pl.when(jnp.logical_not(stays))
            def _():
                send(out_src.at[k, nn], out_got.at[spot], out_send, out_recv, dev(k, 2 * c + nn, z, cd))

    @pl.when(keeps)
    def _():
        wait(out_got.at[pl.ds(0, 7)], out_recv)
        wait(out_got.at[pl.ds(0, 7)], out_send)

    @pl.when(jnp.logical_not(keeps))
    def _():
        wait(out_got, out_recv)
        wait(out_got, out_send)

    for s in range(8):
        basis_ref[:, s * BR : (s + 1) * BR] = out_got[s, 0]
        image_ref[:, s * BR : (s + 1) * BR] = out_got[s, 1]

    wait(zbuf.at[pl.ds(0, 15)], z_send)
    wait(zbuf.at[pl.ds(0, 14)], r_send)
    wait(gd.at[pl.ds(0, 3)], x_send)
    wait(left_all.at[c, pl.ds(0, 15)], l_send.at[0])
    wait(left_all.at[c], l_send.at[1])
    wait(shift_all.at[c, pl.ds(0, 3)], s_send.at[0])
    wait(shift_all.at[c], s_send.at[1])
    for ag in (ag2, ag2b, ag3):
        ag[3]()
    early[4]()
    late[4]()


def per_device(start_vector, precond_diag, left_env, right_env, right_shift, sector_length):
    vmem = pl.BlockSpec(memory_space=pltpu.VMEM)
    smem = pl.BlockSpec(memory_space=pltpu.SMEM)
    hbm = pl.BlockSpec(memory_space=pl.ANY)
    DMA = pltpu.SemaphoreType.DMA
    return pl.pallas_call(
        kernel,
        out_shape=[jax.ShapeDtypeStruct((ROWS, 1024), F32)] * 2,
        in_specs=[hbm, hbm, vmem, hbm, smem, smem],
        out_specs=[vmem, vmem],
        scratch_shapes=[
            pltpu.VMEM((ROWS, NBLK * BR), F32),
            pltpu.VMEM((ROWS, NBLK * BR), F32),
            pltpu.VMEM((NZ, TPD, BR, BR), F32),
            pltpu.VMEM((2, 4, 2, TPD, BR, BR), F32),
            pltpu.VMEM((2, 4, 2, TPD, BR, BR), BF16),
            pltpu.VMEM((2, 4, 2, TPD, BR, BR), BF16),
            pltpu.VMEM((KS, 16, 4, 2) + TILE, F32),
            pltpu.VMEM((3 * KS, 16, 4) + TILE, F32),
            pltpu.VMEM((KS, 16, 4) + TILE, F32),
            pltpu.VMEM((2 * KS, 16, 4) + TILE, F32),
            pltpu.VMEM((KS, 16, 4) + TILE, F32),
            pltpu.VMEM((2, 3 * KS) + TILE, F32),
            pltpu.VMEM((13, KS, 2) + TILE, F32),
            pltpu.VMEM((KS, 2) + TILE, F32),
            pltpu.VMEM((2, 16) + TILE, F32),
            pltpu.VMEM((2, 4) + TILE, jnp.int32),
            pltpu.SMEM((2, 4) + TILE, jnp.int32),
            pltpu.VMEM((TERMS, KS, ROWS) + TILE, F32),
            pltpu.VMEM((KS,) + TILE, F32),
            pltpu.VMEM((16, 24, BR), F32),
            pltpu.VMEM((16, 24, BR), F32),
            pltpu.VMEM((2, 24, BR), F32),
            pltpu.VMEM((16, 16, BR), F32),
            pltpu.VMEM((16, 16, BR), F32),
            pltpu.VMEM((2, 16, BR), F32),
            pltpu.VMEM((KS, 2, 2) + TILE, F32),
            pltpu.VMEM((8, 2) + TILE, F32),
            DMA((3,)),
            DMA,
            DMA((TPD, 8)),
            DMA((TPD, 7)),
            DMA,
            DMA,
            DMA,
            DMA((3,)),
            DMA,
            DMA((2,)),
            DMA((2,)),
            DMA((2,)),
            DMA((2,)),
            DMA,
            DMA((3, 2)),
            DMA((3, 16)),
            DMA((3,)),
            DMA((2, 3)),
            DMA((2, 3)),
            DMA,
            DMA,
        ],
        compiler_params=pltpu.CompilerParams(
            collective_id=0, has_side_effects=True, vmem_limit_bytes=48 * 1024 * 1024
        ),
        cost_estimate=pl.CostEstimate(flops=600_000_000, bytes_accessed=2_000_000, transcendentals=0),
    )(start_vector, precond_diag, left_env, right_env, right_shift, sector_length)


def solution(mesh):
    placed = (
        P("sec", None),
        P("sec", None),
        P("mpo", "sec", None),
        P("mpo", "sec", None),
        P("mpo"),
        P("sec"),
    )
    return jax.shard_map(
        per_device,
        mesh=mesh,
        in_specs=placed,
        out_specs=(P("sec", "mpo"), P("sec", "mpo")),
        check_vma=False,
    )
```

time: 1320 us -> 120 us (0.09)
  blocking collectives: 806 us -> 0 us
  waiting for transfers between devices: 417 us -> 0 us
  Pallas kernels: 0 us -> 114 us
  matrix products: 47.8 us -> 0 us
  between operations: 25.2 us -> 1.33 us
    psum x7 -> x0, blocking collectives: 806 us -> none  [global_sums(): return lax.psum(values, 'sec')]
    psum x3 -> x0, waiting for transfers between devices: 373 us -> none  [apply_operator(): return lax.psum(local_image(vector), 'mpo')]
    pallas_call x0 -> x1, Pallas kernels: none -> 114 us  [per_device(): pl.pallas_call(kernel, out_shape=[jax.ShapeDtypeStruct((ROWS, 1024), F32)...]
    dot_general x18 -> x0, matrix products: 47.8 us -> none  [the longest x9 41.5 us: local_image(): jnp.einsum('inb,nbc->inc', mixed, right_blocks[term_index], precision=lax...]
    all_gather x1 -> x0, waiting for transfers between devices: 43.4 us -> none  [per_device(): gathered = lax.all_gather(right_env, 'sec', axis=1, tiled=True)]
  transfers between devices with their start and end apart: 4 -> 0, of which waited for: 4 -> 0; matrix products, arithmetic and copies ran while one was open for 1% -> 0% of each run, Pallas kernels for 0% -> 0%
where the time goes in v2:
time: 120 us
  Pallas kernels  114 us (95%)
  local copies, waits for them, and re-layouts  4.76 us (4%)
  between operations  1.33 us (1%)
    pallas_call x1, Pallas kernels, per_device(): pl.pallas_call(kernel, out_shape=[jax.ShapeDtypeStruct((ROWS, 1024), F32)...  114 us
    unnamed x12, local copies, waits for them, and re-layouts  4.76 us

profile of v2, /device:TPU:1, one launch (start us, length us, event | category | flops | bytes accessed | tf_op | source)
XLA Modules:
  0.0 119.8 jit_solution(12825925487720803227)
XLA Ops:
  0.6 0.0 copy-start.4
  1.3 0.0 copy-done.4
  1.3 0.0 copy-start
  1.3 0.9 copy-done
  2.3 0.0 copy-start.1
  2.3 0.9 copy-done.1
  3.2 0.0 copy-start.2
  3.2 0.9 copy-done.2
  4.1 0.0 copy-start.3
  4.1 0.7 copy-done.3
  4.8 113.7 %shard_map.77 = (f32[8,1024]{1,0:T(8,128)S(1)}, f32[8,1024]{1,0:T(8,128)S(1)}) custom-call(f32[8,8192]{1,0:T(8,128)S(1)} %copy-done, f32[8,8192]{1,0:T(8,128)S(1)} %copy-done.1, f32[3,8,8]{2,1,0:T(8,128)S(1)} %copy-done.3, f32[3,128,128]{2,1,0:T(8,128)S(1)} %copy-done.2, s32[3]{0:T(128)S(1)} %copy-done.4, s32[1]{0:T(128)S(6)} %copy.10.length_ref), custom_call_target="tpu_custom_call" | custom-call | flops 600000000 | bytes 2000000 | tf_op jit(solution)/shard_map/pallas_call | solution.py:546
  118.5 0.6 copy.11
  119.2 0.6 copy.12
Async XLA Ops:
  0.6 0.7 copy-start.4
  1.3 1.0 copy-start
  2.3 0.9 copy-start.1
  3.2 0.9 copy-start.2
  4.1 0.7 copy-start.3

commit v3 on v2

--- a/solution.py
+++ b/solution.py
@@ -18,25 +18,28 @@
 EPS = 1e-6
 TILE = (ROWS, BR)
 
-G, B, E, H_, Q, S, A_, AA, AQ, P_, T, W, AP = range(13)
+G, B, E, H_, Q, S, A_, AA, P_, PP, T, AP = range(12)
 EARLY = [
-    (G, G), (G, B), (G, A_), (B, B), (A_, B), (A_, A_), (G, H_), (G, Q), (B, Q), (A_, H_), (A_, Q),
-    (E, B), (E, A_), (AA, A_), (E, Q), (AA, Q), (E, E), (E, AA), (AA, AA), (E, AQ), (AA, AQ), (AQ, AQ),
+    (G, G), (G, H_), (G, B), (G, A_), (B, B), (A_, B), (A_, A_), (A_, H_),
+    (E, B), (E, A_), (AA, A_), (E, E), (E, AA), (AA, AA),
 ]
-LATE = [(G, P_), (B, P_), (A_, P_), (E, P_), (AA, P_), (E, AP), (AA, AP), (AQ, AP), (AP, AP)]
+LATE = [(G, PP), (B, PP), (A_, PP), (E, PP), (AA, PP), (E, AP), (AA, AP), (AP, AP)]
 
 
 def kernel(
     start_hbm,
     diag_hbm,
-    left_ref,
+    left_hbm,
     right_hbm,
-    shift_ref,
-    length_ref,
+    shift_hbm,
+    length_hbm,
     basis_ref,
     image_ref,
     start_ref,
     diag_ref,
+    left_ref,
+    shift_ref,
+    length_ref,
     zbuf,
     rbuf,
     r_hi,
@@ -54,12 +57,10 @@
     shift_sm,
     left_wide,
     mask,
-    dz0,
-    dp0,
-    dc0,
-    dz1,
-    dp1,
-    dc1,
+    d_rows,
+    dz,
+    dp,
+    dc,
     out_src,
     out_got,
     in_sem,
@@ -122,6 +123,9 @@
         pltpu.make_async_copy(right_hbm, zbuf.at[z], in_sem.at[0]),
         pltpu.make_async_copy(start_hbm, start_ref, in_sem.at[1]),
         pltpu.make_async_copy(diag_hbm, diag_ref, in_sem.at[2]),
+        pltpu.make_async_copy(left_hbm, left_ref, in_sem.at[3]),
+        pltpu.make_async_copy(shift_hbm, shift_ref, in_sem.at[4]),
+        pltpu.make_async_copy(length_hbm, length_ref, in_sem.at[5]),
     ]
     for load in loads:
         load.start()
@@ -132,6 +136,8 @@
         pl.semaphore_signal(barrier, inc=1, device_id=p, device_id_type=MESH)
 
     sub = lax.broadcasted_iota(jnp.int32, TILE, 0)
+    for load in loads[3:]:
+        load.wait()
     left_all[c, here] = jnp.zeros(TILE, F32)
     for t in range(TPD):
         left_all[c, here, :, t * ROWS : (t + 1) * ROWS] = left_ref[t]
@@ -150,15 +156,16 @@
         nn = lax.rem(lax.div(zz, 4), 2)
         yd, cd = lax.rem(zz, 4), lax.div(zz, 8)
         dst = rbuf.at[nn, y, c, t]
+        sem = r_recv.at[nn]
         stays = jnp.logical_and(yd == y, cd == c)
 
         @pl.when(stays)
         def _():
-            pltpu.make_async_copy(zbuf.at[zz, t], dst, r_recv).start()
+            pltpu.make_async_copy(zbuf.at[zz, t], dst, sem).start()
 
         @pl.when(jnp.logical_not(stays))
         def _():
-            send(zbuf.at[zz, t], dst, r_send, r_recv, dev(x, yd, z, cd))
+            send(zbuf.at[zz, t], dst, r_send, sem, dev(x, yd, z, cd))
 
     for t in range(TPD):
         send(zbuf.at[z, t], zbuf.at[z, t], z_send, z_plus.at[t, 0], up)
@@ -167,8 +174,11 @@
     def half(k, cc):
         return gd.at[k, :, pl.ds(2 * cc, 2)]
 
-    for d in (2, 1, 3):
-        send(half(x, c), half(x, c), x_send, x_recv.at[d - 1], dev(lax.rem(x + d, 4), y, z, c))
+    def send_rows(i):
+        rows = gd.at[x, pl.ds(2 * i, 2), pl.ds(2 * c, 2)]
+        for d in (2, 1, 3):
+            send(rows, rows, x_send, x_recv.at[d - 1], dev(lax.rem(x + d, 4), y, z, c))
+
     for d in range(1, 4):
         send(shift_all.at[c, y], shift_all.at[c, y], s_send.at[0], s_recv.at[0], dev(x, lax.rem(y + d, 4), z, c))
     for o in offsets:
@@ -178,15 +188,20 @@
 
     def ring_step(i, t):
         zp, zm = lax.rem(z + NZ - i, NZ), lax.rem(z + i, NZ)
-        wait(zbuf.at[zp, t], z_plus.at[t, i - 1])
+        top, low = pl.ds(0, BR // 2), pl.ds(BR // 2, BR // 2)
         if i < 8:
-            send(zbuf.at[zp, t], zbuf.at[zp, t], z_send, z_plus.at[t, i], up)
-        deliver(zp, t)
-        if i < 8:
+            wait(zbuf.at[zp, t], z_plus.at[t, i - 1])
+            block = zbuf.at[zp, t] if i < 7 else zbuf.at[zp, t, top]
+            send(block, block, z_send, z_plus.at[t, i], up)
             wait(zbuf.at[zm, t], z_minus.at[t, i - 1])
-            if i < 7:
-                send(zbuf.at[zm, t], zbuf.at[zm, t], z_send, z_minus.at[t, i], down)
+            block = zbuf.at[zm, t] if i < 7 else zbuf.at[zm, t, low]
+            send(block, block, z_send, z_minus.at[t, i], down)
+            deliver(zp, t)
             deliver(zm, t)
+        else:
+            wait(zbuf.at[zp, t, top], z_plus.at[t, 7])
+            wait(zbuf.at[zp, t, low], z_minus.at[t, 7])
+            deliver(zp, t)
 
     def pass_rows(d):
         k = lax.rem(x + 4 - d, 4)
@@ -239,19 +254,23 @@
 
         lax.fori_loop(first, first + count, body, 0)
 
-    idle = [lambda: None]
-    tasks = idle * 3 + [pass_small] + idle + [take_small]
-    tasks += [lambda i=i: widen(4 * i, 4) for i in range(8)]
-    tasks += [lambda: pass_rows(1), lambda: pass_rows(3), lambda: pass_rows(2), take_rows]
-    tasks += [lambda i=i: vectors(3 * i, 3) for i in range(5)] + [lambda: vectors(15, 1)]
-    tasks = tasks[::-1]
+    tasks = {i: [lambda i=i: send_rows(i)] for i in range(8)}
+    tasks[4].append(pass_small)
+    tasks[6].append(take_small)
+    for i in range(8):
+        tasks.setdefault(i + 7, []).append(lambda i=i: widen(4 * i, 4))
+    tasks[15] = [lambda: pass_rows(1)]
+    tasks[16] = [lambda: pass_rows(3)]
+    tasks[17] = [lambda: pass_rows(2)]
+    tasks[18] = [take_rows, lambda: vectors(0, 2)]
+    for i in range(19, 23):
+        tasks[i] = [lambda i=i: vectors(3 * i - 55, 3)]
+    tasks[23] = [lambda: vectors(14, 2)]
     for i in range(1, 9):
         for t in range(TPD):
             ring_step(i, t)
-            if tasks:
-                tasks.pop()()
-    while tasks:
-        tasks.pop()()
+            for task in tasks.get((i - 1) * TPD + t, []):
+                task()
 
     for nn in range(2):
         for k in range(KS):
@@ -261,17 +280,18 @@
             piece[B, k, nn] = v1[KS + k, here, j]
             piece[E, k, nn] = v1[2 * KS + k, here, j]
     to_sm.wait()
-    wait(rbuf, r_recv)
-
-    def product(v, nk, cut):
+
+    def product(v, nk, cut=False, only=None):
         rows = nk * ROWS
-        y_sum[:, pl.ds(0, nk)] = jnp.zeros((2, nk) + TILE, F32)
+        blocks = range(2) if only is None else (only,)
+        for nn in blocks:
+            y_sum[nn, pl.ds(0, nk)] = jnp.zeros((nk,) + TILE, F32)
 
         def body(i, carry):
             yy, rest = lax.div(i, 2 * TPD), lax.rem(i, 2 * TPD)
             cc, t = lax.div(rest, TPD), lax.rem(rest, TPD)
             shift = shift_sm[cc, yy, t, 0]
-            for nn in range(2):
+            for nn in blocks:
                 m = 16 * (2 * c + nn) + here + shift
                 m = jnp.where(m >= NBLK, m - NBLK, m)
                 r, j4 = lax.rem(m, 16), lax.div(m, 16)
@@ -311,8 +331,8 @@
                 send(at(here, c), at(here, c), ag_send.at[phase, 0], ag_recv.at[phase, o], peer(o))
             send(at(here, c), at(here, c), ag_send.at[phase, 1], ag_core.at[phase], other)
 
-        def pass_on():
-            for o in offsets[::-1]:
+        def pass_on(first, last):
+            for o in offsets[::-1][first:last]:
                 r = sender(o)
                 wait(at(r, c), ag_recv.at[phase, o])
                 send(at(r, c), at(r, c), ag_send.at[phase, 1], ag_core.at[phase], other)
@@ -326,123 +346,126 @@
 
         return start, pass_on, finish, sent
 
-    def dots(g, dz, dp, dc):
+    def dots(g):
         def start(pairs):
-            dz[z] = jnp.zeros(dz.shape[1:], F32)
+            d_rows[g] = jnp.zeros((16, BR), F32)
             for r, (a, b) in enumerate(pairs):
                 prod = (piece[a] * piece[b]).reshape((2 * KS,) + TILE)
-                dz[z, r : r + 1, :] = jnp.sum(jnp.sum(prod, axis=0), axis=0, keepdims=True)
+                d_rows[g, r : r + 1, :] = jnp.sum(jnp.sum(prod, axis=0), axis=0, keepdims=True)
+            total = jnp.broadcast_to(jnp.sum(d_rows[g], axis=1, keepdims=True), (16, BR))
+            at_row = lax.broadcasted_iota(jnp.int32, (16, BR), 0) == lax.broadcasted_iota(jnp.int32, (16, BR), 1)
+            dz[g, z] = jnp.sum(jnp.where(at_row, total, 0.0), axis=0, keepdims=True)
             for p in zdevs:
-                send(dz.at[z], dz.at[z], dot_send.at[g, 0], dot_recv.at[g, 0], p)
+                send(dz.at[g, z], dz.at[g, z], dot_send.at[g, 0], dot_recv.at[g, 0], p)
 
         def plane():
-            wait(dz.at[pl.ds(0, 15)], dot_recv.at[g, 0])
-            dp[here] = jnp.sum(dz[...], axis=0)
+            wait(dz.at[g, pl.ds(0, 15)], dot_recv.at[g, 0])
+            dp[g, here] = jnp.sum(dz[g], axis=0)
             for o in offsets:
-                send(dp.at[here], dp.at[here], dot_send.at[g, 1], dot_recv.at[g, 1], peer(o))
+                send(dp.at[g, here], dp.at[g, here], dot_send.at[g, 1], dot_recv.at[g, 1], peer(o))
 
         def core():
-            wait(dp.at[pl.ds(0, 15)], dot_recv.at[g, 1])
-            dc[c] = jnp.sum(dp[...], axis=0)
-            send(dc.at[c], dc.at[c], dot_send.at[g, 2], dot_recv.at[g, 2], other)
+            wait(dp.at[g, pl.ds(0, 15)], dot_recv.at[g, 1])
+            dc[g, c] = jnp.sum(dp[g], axis=0)
+            send(dc.at[g, c], dc.at[g, c], dot_send.at[g, 2], dot_recv.at[g, 2], other)
 
         def done(pairs):
-            wait(dc.at[1 - c], dot_recv.at[g, 2])
-            total = jnp.sum(dc[0] + dc[1], axis=1, keepdims=True)
-            return {p: jnp.broadcast_to(total[r : r + 1, :], TILE) for r, p in enumerate(pairs)}
+            wait(dc.at[g, 1 - c], dot_recv.at[g, 2])
+            total = dc[g, 0] + dc[g, 1]
+            return {p: jnp.broadcast_to(total[:, r : r + 1], TILE) for r, p in enumerate(pairs)}
 
         def sent():
-            wait(dz.at[pl.ds(0, 15)], dot_send.at[g, 0])
-            wait(dp.at[pl.ds(0, 15)], dot_send.at[g, 1])
-            wait(dc.at[c], dot_send.at[g, 2])
+            wait(dz.at[g, pl.ds(0, 15)], dot_send.at[g, 0])
+            wait(dp.at[g, pl.ds(0, 15)], dot_send.at[g, 1])
+            wait(dc.at[g, c], dot_send.at[g, 2])
 
         return start, plane, core, done, sent
 
-    product(v1, 3 * KS, True)
+    apart = lax.rem(y + 8 * c - z + NZ, NZ)
+    near = 1 - lax.div(lax.rem(apart + 9, NZ) + 9, NZ)
+    for nn in (near, 1 - near):
+        wait(rbuf.at[nn], r_recv.at[nn])
+        product(v1, 3 * KS, True, nn)
     mine = pl.ds(2 * c, 2)
     for nn in range(2):
         for k in range(KS):
             h = y_sum[nn, k] * mask[k]
-            q = y_sum[nn, KS + k] * mask[k]
             a = h * inv[k, nn]
             piece[H_, k, nn] = h
-            piece[Q, k, nn] = q
+            piece[Q, k, nn] = y_sum[nn, KS + k] * mask[k]
             piece[S, k, nn] = y_sum[nn, 2 * KS + k] * mask[k]
             piece[A_, k, nn] = a
             piece[AA, k, nn] = a * inv[k, nn]
-            piece[AQ, k, nn] = q * inv[k, nn]
     v2[:, here, mine] = piece[A_]
-    v2b[pl.ds(0, KS), here, mine] = piece[AA]
-    v2b[pl.ds(KS, KS), here, mine] = piece[AQ]
+    v2b[:, here, mine] = piece[AA]
     ag2, ag2b, ag3 = gather(0, v2), gather(1, v2b), gather(2, v3)
-    early, late = dots(0, dz0, dp0, dc0), dots(1, dz1, dp1, dc1)
+    early, late = dots(0), dots(1)
     ag2[0]()
     early[0](EARLY)
+    ag2[1](0, 10)
+    early[1]()
+    ag2[1](10, 15)
     ag2b[0]()
-    ag2[1]()
     ag2[2]()
 
-    product(v2, KS, False)
+    product(v2, KS)
+    early[2]()
+    dot = early[3](EARLY)
+    f1 = jnp.sqrt(CELLS / (dot[G, G] + EPS))
+    r1 = f1 * f1 * dot[G, H_] / CELLS
     for nn in range(2):
         for k in range(KS):
             p = y_sum[nn, k] * mask[k]
+            pp = p - r1 * piece[Q, k, nn]
             piece[P_, k, nn] = p
-            piece[AP, k, nn] = p * inv[k, nn]
+            piece[PP, k, nn] = pp
+            piece[AP, k, nn] = pp * inv[k, nn]
     v3[:, here, mine] = piece[AP]
     ag3[0]()
     late[0](LATE)
-    early[1]()
-    ag2b[1]()
+    ag2b[1](0, 15)
     ag2b[2]()
-    product(v2b, 2 * KS, False)
+    product(v2b, KS)
     for nn in range(2):
         for k in range(KS):
             piece[T, k, nn] = y_sum[nn, k] * mask[k]
-            piece[W, k, nn] = y_sum[nn, KS + k] * mask[k]
-    early[2]()
-    ag3[1]()
+    ag3[1](0, 10)
     late[1]()
+    ag3[1](10, 15)
     ag3[2]()
 
-    product(v3, KS, False)
+    product(v3, KS)
     late[2]()
-    dot = early[3](EARLY)
     dot.update(late[3](LATE))
     dot.update({(b, a): value for (a, b), value in dot.items()})
 
-    f1 = jnp.sqrt(CELLS / (dot[G, G] + EPS))
-    r1 = f1 * f1 * dot[G, H_] / CELLS
     c1 = f1 * f1 * (dot[G, A_] - r1 * dot[G, B]) / CELLS
     w = (-f1 * c1, -f1 * r1, f1)
+    wy = (w[0], f1)
     x_x = [[dot[i, j] for j in (G, B, A_)] for i in (G, B, A_)]
-    x_y = [
-        [dot[G, H_], dot[G, Q], dot[G, P_]],
-        [dot[G, A_], dot[B, Q], dot[B, P_]],
-        [dot[A_, H_], dot[A_, Q], dot[A_, P_]],
-    ]
-    ax_y = [
-        [dot[G, A_], dot[B, Q], dot[B, P_]],
-        [dot[A_, B], dot[E, Q], dot[E, P_]],
-        [dot[A_, A_], dot[AA, Q], dot[AA, P_]],
-    ]
+    x_y = [[dot[G, H_], dot[G, PP]], [dot[G, A_], dot[B, PP]], [dot[A_, H_], dot[A_, PP]]]
+    ax_y = [[dot[G, A_], dot[B, PP]], [dot[A_, B], dot[E, PP]], [dot[A_, A_], dot[AA, PP]]]
     ax_x = [
         [dot[G, B], dot[B, B], dot[A_, B]],
         [dot[B, B], dot[E, B], dot[E, A_]],
         [dot[A_, B], dot[E, A_], dot[AA, A_]],
     ]
 
-    def along(row):
-        return w[0] * row[0] + w[1] * row[1] + w[2] * row[2]
-
-    def form(m):
-        return along([along(row) for row in m])
+    def along(weights, row):
+        total = weights[0] * row[0]
+        for weight, value in zip(weights[1:], row[1:], strict=True):
+            total = total + weight * value
+        return total
+
+    def form(weights, m):
+        return along(w, [along(weights, row) for row in m])
 
     def column(m, j):
         return [row[j] for row in m]
 
-    uu, uk, uak, uau = form(x_x), form(x_y), form(ax_y), form(ax_x)
-    gu, gk, uh = along(x_x[0]), along(x_y[0]), along(column(x_y, 0))
-    gak, gau, uah = along(x_y[1]), along(x_x[1]), along(column(x_x, 2))
+    uu, uk, uak, uau = form(w, x_x), form(wy, x_y), form(wy, ax_y), form(w, ax_x)
+    gu, gk, uh = along(w, x_x[0]), along(wy, x_y[0]), along(w, column(x_y, 0))
+    gak, gau, uah = along(wy, x_y[1]), along(w, x_x[1]), along(w, column(x_x, 2))
     f2 = jnp.sqrt(CELLS / (jnp.maximum(uu, 0.0) + EPS))
     b_ = f1 * f2 * (gk + uh) / (2.0 * CELLS)
     d_ = f2 * f2 * uk / CELLS
@@ -465,11 +488,9 @@
         B: -ritz * (n1 + n2 * w[0]),
         E: -ritz * n2 * w[1],
         AA: -ritz * n2 * w[2],
-        AQ: n2 * w[1],
-        AP: n2 * w[2],
+        AP: n2 * f1,
     }
-    dot[A_, AQ], dot[A_, AP], dot[B, AQ], dot[B, AP] = dot[AA, Q], dot[AA, P_], dot[E, Q], dot[E, P_]
-    dot[B, AA] = dot[E, A_]
+    dot[A_, AP], dot[B, AP], dot[B, AA] = dot[AA, PP], dot[E, PP], dot[E, A_]
     dot.update({(b, a): value for (a, b), value in dot.items()})
     tt = jnp.zeros(TILE, F32)
     for i in t2:
@@ -485,7 +506,7 @@
     coef[B] = coef[B] - e2 * f2 * w[1]
     coef[A_] = coef[A_] - e2 * f2 * w[2]
     coef = {i: f3 * value for i, value in coef.items()}
-    image_of = {A_: P_, B: Q, E: S, AA: T, AQ: W, G: H_}
+    image_of = {A_: P_, B: Q, E: S, AA: T, G: H_}
     for nn in range(2):
         for k in range(KS):
             basis = coef[AP] * piece[AP, k, nn]
@@ -540,17 +561,19 @@
 
 def per_device(start_vector, precond_diag, left_env, right_env, right_shift, sector_length):
     vmem = pl.BlockSpec(memory_space=pltpu.VMEM)
-    smem = pl.BlockSpec(memory_space=pltpu.SMEM)
-    hbm = pl.BlockSpec(memory_space=pl.ANY)
+    hbm = pl.BlockSpec(memory_space=pltpu.HBM)
     DMA = pltpu.SemaphoreType.DMA
     return pl.pallas_call(
         kernel,
         out_shape=[jax.ShapeDtypeStruct((ROWS, 1024), F32)] * 2,
-        in_specs=[hbm, hbm, vmem, hbm, smem, smem],
+        in_specs=[hbm] * 6,
         out_specs=[vmem, vmem],
         scratch_shapes=[
             pltpu.VMEM((ROWS, NBLK * BR), F32),
             pltpu.VMEM((ROWS, NBLK * BR), F32),
+            pltpu.VMEM((TPD, ROWS, ROWS), F32),
+            pltpu.SMEM((TPD,), jnp.int32),
+            pltpu.SMEM((1,), jnp.int32),
             pltpu.VMEM((NZ, TPD, BR, BR), F32),
             pltpu.VMEM((2, 4, 2, TPD, BR, BR), F32),
             pltpu.VMEM((2, 4, 2, TPD, BR, BR), BF16),
@@ -558,30 +581,28 @@
             pltpu.VMEM((KS, 16, 4, 2) + TILE, F32),
             pltpu.VMEM((3 * KS, 16, 4) + TILE, F32),
             pltpu.VMEM((KS, 16, 4) + TILE, F32),
-            pltpu.VMEM((2 * KS, 16, 4) + TILE, F32),
+            pltpu.VMEM((KS, 16, 4) + TILE, F32),
             pltpu.VMEM((KS, 16, 4) + TILE, F32),
             pltpu.VMEM((2, 3 * KS) + TILE, F32),
-            pltpu.VMEM((13, KS, 2) + TILE, F32),
+            pltpu.VMEM((12, KS, 2) + TILE, F32),
             pltpu.VMEM((KS, 2) + TILE, F32),
             pltpu.VMEM((2, 16) + TILE, F32),
             pltpu.VMEM((2, 4) + TILE, jnp.int32),
             pltpu.SMEM((2, 4) + TILE, jnp.int32),
             pltpu.VMEM((TERMS, KS, ROWS) + TILE, F32),
             pltpu.VMEM((KS,) + TILE, F32),
-            pltpu.VMEM((16, 24, BR), F32),
-            pltpu.VMEM((16, 24, BR), F32),
-            pltpu.VMEM((2, 24, BR), F32),
-            pltpu.VMEM((16, 16, BR), F32),
-            pltpu.VMEM((16, 16, BR), F32),
             pltpu.VMEM((2, 16, BR), F32),
+            pltpu.VMEM((2, 16, 1, BR), F32),
+            pltpu.VMEM((2, 16, 1, BR), F32),
+            pltpu.VMEM((2, 2, 1, BR), F32),
             pltpu.VMEM((KS, 2, 2) + TILE, F32),
             pltpu.VMEM((8, 2) + TILE, F32),
-            DMA((3,)),
+            DMA((6,)),
             DMA,
             DMA((TPD, 8)),
-            DMA((TPD, 7)),
+            DMA((TPD, 8)),
             DMA,
-            DMA,
+            DMA((2,)),
             DMA,
             DMA((3,)),
             DMA,
@@ -599,7 +620,7 @@
             DMA,
         ],
         compiler_params=pltpu.CompilerParams(
-            collective_id=0, has_side_effects=True, vmem_limit_bytes=48 * 1024 * 1024
+            collective_id=0, has_side_effects=True, vmem_limit_bytes=60 * 1024 * 1024
         ),
         cost_estimate=pl.CostEstimate(flops=600_000_000, bytes_accessed=2_000_000, transcendentals=0),
     )(start_vector, precond_diag, left_env, right_env, right_shift, sector_length)

time: 120 us -> 104 us (0.87)
  Pallas kernels: 114 us -> 100 us
  local copies, waits for them, and re-layouts: 4.76 us -> 2 us
    pallas_call x1, Pallas kernels: 114 us -> 100 us  [per_device(): pl.pallas_call(kernel, out_shape=[jax.ShapeDtypeStruct((ROWS, 1024), F32)...]
    unnamed x12 -> x4, local copies, waits for them, and re-layouts: 4.76 us -> 2 us
where the time goes in v3:
time: 104 us; the launch traced here: 103 us
  Pallas kernels  100 us (96%)
  local copies, waits for them, and re-layouts  2 us (2%)
  between operations  1.29 us (1%)
    pallas_call x1, Pallas kernels, per_device(): pl.pallas_call(kernel, out_shape=[jax.ShapeDtypeStruct((ROWS, 1024), F32)...  100 us

profile of v3, /device:TPU:1, one launch (start us, length us, event | category | flops | bytes accessed | tf_op | source)
XLA Modules:
  0.0 103.4 jit_solution(3462084315397597818)
XLA Ops:
  1.3 100.2 %shard_map.77 = (f32[8,1024]{1,0:T(8,128)}, f32[8,1024]{1,0:T(8,128)}) custom-call(f32[8,8192]{1,0:T(8,128)} %start_hbm.1, f32[8,8192]{1,0:T(8,128)} %diag_hbm.1, f32[3,8,8]{2,1,0:T(8,128)} %left_hbm.1, f32[3,128,128]{2,1,0:T(8,128)} %right_hbm.1, s32[3]{0:T(128)} %shift_hbm.1, s32[1]{0:T(128)S(6)} %copy.10.length_hbm), custom_call_target="tpu_custom_call" | custom-call | flops 600000000 | bytes 2000000 | tf_op jit(solution)/shard_map/pallas_call | solution.py:566
  101.4 0.0 copy-start
  101.4 1.4 %copy.11 = f32[8,1024]{1,0:T(8,128)} copy(f32[8,1024]{1,0:T(8,128)} %get-tuple-element.4) | data formatting | bytes 65536
  102.8 0.0 copy-done
  102.8 0.6 copy.12
Async XLA Ops:
  101.4 1.4 %copy-start = (f32[8,1024]{1,0:T(8,128)S(1)}, f32[8,1024]{1,0:T(8,128)}, u32[]{:S(2)}) copy-start(f32[8,1024]{1,0:T(8,128)} %get-tuple-element.5) | copy-start | bytes 98308

commit v4 on v3

--- a/solution.py
+++ b/solution.py
@@ -18,7 +18,7 @@
 EPS = 1e-6
 TILE = (ROWS, BR)
 
-G, B, E, H_, Q, S, A_, AA, P_, PP, T, AP = range(12)
+G, B, E, H_, Q, A_, AA, PP, AP = range(9)
 EARLY = [
     (G, G), (G, H_), (G, B), (G, A_), (B, B), (A_, B), (A_, A_), (A_, H_),
     (E, B), (E, A_), (AA, A_), (E, E), (E, AA), (AA, AA),
@@ -49,6 +49,7 @@
     v2,
     v2b,
     v3,
+    mixed,
     y_sum,
     piece,
     inv,
@@ -61,8 +62,12 @@
     dz,
     dp,
     dc,
-    out_src,
-    out_got,
+    qs_src,
+    qs_got,
+    t_src,
+    t_got,
+    o_src,
+    o_got,
     in_sem,
     z_send,
     z_plus,
@@ -156,7 +161,7 @@
         nn = lax.rem(lax.div(zz, 4), 2)
         yd, cd = lax.rem(zz, 4), lax.div(zz, 8)
         dst = rbuf.at[nn, y, c, t]
-        sem = r_recv.at[nn]
+        sem = r_recv.at[nn, lax.rem(yd - y + 4, 4)]
         stays = jnp.logical_and(yd == y, cd == c)
 
         @pl.when(stays)
@@ -254,18 +259,76 @@
 
         lax.fori_loop(first, first + count, body, 0)
 
+    def mix(v, nk, first, count, step):
+        rows = nk * ROWS
+
+        def body(at, carry):
+            for u in range(step):
+                i = first + at * step + u
+                yy, rest = lax.div(i, 2 * TPD), lax.rem(i, 2 * TPD)
+                shift = shift_sm[lax.div(rest, TPD), yy, lax.rem(rest, TPD), 0]
+                for nn in range(2):
+                    m = 16 * (2 * c + nn) + here + shift
+                    m = jnp.where(m >= NBLK, m - NBLK, m)
+                    r, j4 = lax.rem(m, 16), lax.div(m, 16)
+                    tiles = []
+                    for k in range(nk):
+                        src = v[k, r, j4]
+                        total = None
+                        for j in range(ROWS):
+                            term = left_wide[i, k % KS, j] * src[j : j + 1, :]
+                            total = term if total is None else total + term
+                        tiles.append(total)
+                    p = jnp.concatenate(tiles, axis=0)
+                    hi = p.astype(BF16)
+                    mixed[i, nn, 0:rows] = hi
+                    mixed[i, nn, rows : 2 * rows] = (p - hi.astype(F32)).astype(BF16)
+            return carry
+
+        lax.fori_loop(0, count // step, body, 0)
+
+    def terms_of(nn, yy, rows, cut):
+        acc = None
+        for q in range(2 * TPD):
+            cc, t = q // TPD, q % TPD
+            if cut:
+                full = rbuf[nn, yy, cc, t]
+                rh = full.astype(BF16)
+                rl = (full - rh.astype(F32)).astype(BF16)
+                r_hi[nn, yy, cc, t] = rh
+                r_lo[nn, yy, cc, t] = rl
+            else:
+                rh = r_hi[nn, yy, cc, t]
+                rl = r_lo[nn, yy, cc, t]
+            i = yy * 2 * TPD + q
+            both = jnp.dot(mixed[i, nn, 0 : 2 * rows], rh, preferred_element_type=F32)
+            more = jnp.dot(mixed[i, nn, 0:rows], rl, preferred_element_type=F32)
+            res = both[:rows] + both[rows:] + more
+            acc = res if acc is None else acc + res
+        return acc
+
+    def product(v, nk):
+        mix(v, nk, 0, TERMS, 4)
+        for nn in range(2):
+            acc = terms_of(nn, 0, nk * ROWS, False)
+            for yy in range(1, 4):
+                acc = acc + terms_of(nn, yy, nk * ROWS, False)
+            y_sum[nn, pl.ds(0, nk)] = acc.reshape((nk,) + TILE)
+
     tasks = {i: [lambda i=i: send_rows(i)] for i in range(8)}
     tasks[4].append(pass_small)
     tasks[6].append(take_small)
-    for i in range(8):
-        tasks.setdefault(i + 7, []).append(lambda i=i: widen(4 * i, 4))
-    tasks[15] = [lambda: pass_rows(1)]
-    tasks[16] = [lambda: pass_rows(3)]
-    tasks[17] = [lambda: pass_rows(2)]
-    tasks[18] = [take_rows, lambda: vectors(0, 2)]
-    for i in range(19, 23):
-        tasks[i] = [lambda i=i: vectors(3 * i - 55, 3)]
-    tasks[23] = [lambda: vectors(14, 2)]
+    for i in range(4):
+        tasks.setdefault(i + 7, []).append(lambda i=i: widen(8 * i, 8))
+    tasks[11] = [lambda: pass_rows(1)]
+    tasks[12] = [lambda: pass_rows(3)]
+    tasks[13] = [lambda: pass_rows(2)]
+    tasks[14] = [take_rows, lambda: vectors(0, 4)]
+    for i in range(15, 18):
+        tasks[i] = [lambda i=i: vectors(4 * i - 56, 4)]
+    tasks[17].append(to_sm.wait)
+    for i in range(18, 24):
+        tasks[i] = [lambda i=i: mix(v1, 3 * KS, 4 * i - 72, 4, 1)]
     for i in range(1, 9):
         for t in range(TPD):
             ring_step(i, t)
@@ -279,57 +342,16 @@
             piece[G, k, nn] = v1[k, here, j]
             piece[B, k, nn] = v1[KS + k, here, j]
             piece[E, k, nn] = v1[2 * KS + k, here, j]
-    to_sm.wait()
-
-    def product(v, nk, cut=False, only=None):
-        rows = nk * ROWS
-        blocks = range(2) if only is None else (only,)
-        for nn in blocks:
-            y_sum[nn, pl.ds(0, nk)] = jnp.zeros((nk,) + TILE, F32)
-
-        def body(i, carry):
-            yy, rest = lax.div(i, 2 * TPD), lax.rem(i, 2 * TPD)
-            cc, t = lax.div(rest, TPD), lax.rem(rest, TPD)
-            shift = shift_sm[cc, yy, t, 0]
-            for nn in blocks:
-                m = 16 * (2 * c + nn) + here + shift
-                m = jnp.where(m >= NBLK, m - NBLK, m)
-                r, j4 = lax.rem(m, 16), lax.div(m, 16)
-                tiles = []
-                for k in range(nk):
-                    src = v[k, r, j4]
-                    total = None
-                    for j in range(ROWS):
-                        term = left_wide[i, k % KS, j] * src[j : j + 1, :]
-                        total = term if total is None else total + term
-                    tiles.append(total)
-                p = jnp.concatenate(tiles, axis=0)
-                hi = p.astype(BF16)
-                lo = (p - hi.astype(F32)).astype(BF16)
-                if cut:
-                    full = rbuf[nn, yy, cc, t]
-                    rh = full.astype(BF16)
-                    rl = (full - rh.astype(F32)).astype(BF16)
-                    r_hi[nn, yy, cc, t] = rh
-                    r_lo[nn, yy, cc, t] = rl
-                else:
-                    rh = r_hi[nn, yy, cc, t]
-                    rl = r_lo[nn, yy, cc, t]
-                both = jnp.dot(jnp.concatenate([hi, lo], axis=0), rh, preferred_element_type=F32)
-                more = jnp.dot(hi, rl, preferred_element_type=F32)
-                y_sum[nn, pl.ds(0, nk)] += (both[:rows] + both[rows:] + more).reshape((nk,) + TILE)
-            return carry
-
-        lax.fori_loop(0, TERMS, body, 0)
 
     def gather(phase, v):
         def at(r, cc):
             return v.at[:, r, pl.ds(2 * cc, 2)]
 
-        def start():
+        def start(nn):
+            half = v.at[:, here, pl.ds(2 * c + nn, 1)]
             for o in offsets:
-                send(at(here, c), at(here, c), ag_send.at[phase, 0], ag_recv.at[phase, o], peer(o))
-            send(at(here, c), at(here, c), ag_send.at[phase, 1], ag_core.at[phase], other)
+                send(half, half, ag_send.at[phase, 0], ag_recv.at[phase, o], peer(o))
+            send(half, half, ag_send.at[phase, 1], ag_core.at[phase], other)
 
         def pass_on(first, last):
             for o in offsets[::-1][first:last]:
@@ -381,31 +403,70 @@
 
         return start, plane, core, done, sent
 
+    spot = 4 * lax.rem(y, 2) + x
+    cd = lax.div(y, 2)
+    keeps = cd == c
+
+    def exchange(i, src, got):
+        def start():
+            for k in range(KS):
+                for nn in range(2):
+                    stays = jnp.logical_and(jnp.logical_and(x == k, y == 2 * c + nn), keeps)
+
+                    @pl.when(stays)
+                    def _():
+                        got[spot] = src[k, nn]
+
+                    @pl.when(jnp.logical_not(stays))
+                    def _():
+                        where = dev(k, 2 * c + nn, z, cd)
+                        send(src.at[k, nn], got.at[spot], out_send.at[i], out_recv.at[i], where)
+
+        def arrived(sem):
+            @pl.when(keeps)
+            def _():
+                wait(got.at[pl.ds(0, 7)], sem.at[i])
+
+            @pl.when(jnp.logical_not(keeps))
+            def _():
+                wait(got, sem.at[i])
+
+        return start, lambda: arrived(out_recv), lambda: arrived(out_send)
+
+    ex_early, ex_t, ex_o = exchange(0, qs_src, qs_got), exchange(1, t_src, t_got), exchange(2, o_src, o_got)
+    ag2, ag2b, ag3 = gather(0, v2), gather(1, v2b), gather(2, v3)
+    early, late = dots(0), dots(1)
+
     apart = lax.rem(y + 8 * c - z + NZ, NZ)
     near = 1 - lax.div(lax.rem(apart + 9, NZ) + 9, NZ)
     for nn in (near, 1 - near):
-        wait(rbuf.at[nn], r_recv.at[nn])
-        product(v1, 3 * KS, True, nn)
-    mine = pl.ds(2 * c, 2)
-    for nn in range(2):
+        acc = None
+        for d in (0, 1, 3, 2):
+            yy = lax.rem(y - d + 4, 4)
+            wait(rbuf.at[nn, yy], r_recv.at[nn, d])
+            part = terms_of(nn, yy, 3 * KS * ROWS, True)
+            acc = part if acc is None else acc + part
+        acc = acc.reshape((3 * KS,) + TILE)
         for k in range(KS):
-            h = y_sum[nn, k] * mask[k]
+            h = acc[k] * mask[k]
             a = h * inv[k, nn]
             piece[H_, k, nn] = h
-            piece[Q, k, nn] = y_sum[nn, KS + k] * mask[k]
-            piece[S, k, nn] = y_sum[nn, 2 * KS + k] * mask[k]
             piece[A_, k, nn] = a
+            v2[k, here, 2 * c + nn] = a
             piece[AA, k, nn] = a * inv[k, nn]
-    v2[:, here, mine] = piece[A_]
-    v2b[:, here, mine] = piece[AA]
-    ag2, ag2b, ag3 = gather(0, v2), gather(1, v2b), gather(2, v3)
-    early, late = dots(0), dots(1)
-    ag2[0]()
+            v2b[k, here, 2 * c + nn] = a * inv[k, nn]
+            q = acc[KS + k] * mask[k]
+            piece[Q, k, nn] = q
+            qs_src[k, nn, 0] = q
+            qs_src[k, nn, 1] = acc[2 * KS + k] * mask[k]
+        ag2[0](nn)
     early[0](EARLY)
     ag2[1](0, 10)
     early[1]()
+    ag2b[0](0)
+    ag2b[0](1)
+    ex_early[0]()
     ag2[1](10, 15)
-    ag2b[0]()
     ag2[2]()
 
     product(v2, KS)
@@ -415,26 +476,29 @@
     r1 = f1 * f1 * dot[G, H_] / CELLS
     for nn in range(2):
         for k in range(KS):
-            p = y_sum[nn, k] * mask[k]
-            pp = p - r1 * piece[Q, k, nn]
-            piece[P_, k, nn] = p
+            pp = y_sum[nn, k] * mask[k] - r1 * piece[Q, k, nn]
             piece[PP, k, nn] = pp
             piece[AP, k, nn] = pp * inv[k, nn]
-    v3[:, here, mine] = piece[AP]
-    ag3[0]()
+            v3[k, here, 2 * c + nn] = pp * inv[k, nn]
+        ag3[0](nn)
     late[0](LATE)
     ag2b[1](0, 15)
     ag2b[2]()
     product(v2b, KS)
     for nn in range(2):
         for k in range(KS):
-            piece[T, k, nn] = y_sum[nn, k] * mask[k]
+            t_src[k, nn] = y_sum[nn, k] * mask[k]
+    ex_t[0]()
     ag3[1](0, 10)
     late[1]()
     ag3[1](10, 15)
     ag3[2]()
 
     product(v3, KS)
+    for nn in range(2):
+        for k in range(KS):
+            o_src[k, nn] = y_sum[nn, k] * mask[k]
+    ex_o[0]()
     late[2]()
     dot.update(late[3](LATE))
     dot.update({(b, a): value for (a, b), value in dot.items()})
@@ -506,45 +570,18 @@
     coef[B] = coef[B] - e2 * f2 * w[1]
     coef[A_] = coef[A_] - e2 * f2 * w[2]
     coef = {i: f3 * value for i, value in coef.items()}
-    image_of = {A_: P_, B: Q, E: S, AA: T, G: H_}
-    for nn in range(2):
-        for k in range(KS):
-            basis = coef[AP] * piece[AP, k, nn]
-            image = coef[AP] * (y_sum[nn, k] * mask[k])
-            for i in image_of:
-                basis = basis + coef[i] * piece[i, k, nn]
-                image = image + coef[i] * piece[image_of[i], k, nn]
-            out_src[k, nn, 0] = basis
-            out_src[k, nn, 1] = image
-
-    spot = 4 * lax.rem(y, 2) + x
-    cd = lax.div(y, 2)
-    keeps = cd == c
-    for k in range(KS):
-        for nn in range(2):
-            stays = jnp.logical_and(jnp.logical_and(x == k, y == 2 * c + nn), keeps)
-
-            @pl.when(stays)
-            def _():
-                out_got[spot] = out_src[k, nn]
-
-            @pl.when(jnp.logical_not(stays))
-            def _():
-                send(out_src.at[k, nn], out_got.at[spot], out_send, out_recv, dev(k, 2 * c + nn, z, cd))
-
-    @pl.when(keeps)
-    def _():
-        wait(out_got.at[pl.ds(0, 7)], out_recv)
-        wait(out_got.at[pl.ds(0, 7)], out_send)
-
-    @pl.when(jnp.logical_not(keeps))
-    def _():
-        wait(out_got, out_recv)
-        wait(out_got, out_send)
-
-    for s in range(8):
-        basis_ref[:, s * BR : (s + 1) * BR] = out_got[s, 0]
-        image_ref[:, s * BR : (s + 1) * BR] = out_got[s, 1]
+    coef_q = coef[B] + coef[A_] * r1
+    for ex in (ex_early, ex_t, ex_o):
+        ex[1]()
+    for i in range(8):
+        r = 8 * c + i
+        a, ap, d = v2[x, r, y], v3[x, r, y], gd[x, r, y, 1]
+        basis = coef[AP] * ap + coef[A_] * a + coef[AA] * v2b[x, r, y]
+        basis = basis + coef[G] * v1[x, r, y] + coef[B] * v1[KS + x, r, y] + coef[E] * v1[2 * KS + x, r, y]
+        image = coef[AP] * o_got[i] + (coef[A_] * ap + coef[G] * a) * d
+        image = image + coef_q * qs_got[i, 0] + coef[E] * qs_got[i, 1] + coef[AA] * t_got[i]
+        basis_ref[:, i * BR : (i + 1) * BR] = basis
+        image_ref[:, i * BR : (i + 1) * BR] = image
 
     wait(zbuf.at[pl.ds(0, 15)], z_send)
     wait(zbuf.at[pl.ds(0, 14)], r_send)
@@ -557,6 +594,8 @@
         ag[3]()
     early[4]()
     late[4]()
+    for ex in (ex_early, ex_t, ex_o):
+        ex[2]()
 
 
 def per_device(start_vector, precond_diag, left_env, right_env, right_shift, sector_length):
@@ -583,8 +622,9 @@
             pltpu.VMEM((KS, 16, 4) + TILE, F32),
             pltpu.VMEM((KS, 16, 4) + TILE, F32),
             pltpu.VMEM((KS, 16, 4) + TILE, F32),
+            pltpu.VMEM((TERMS, 2, 6 * KS * ROWS, BR), BF16),
             pltpu.VMEM((2, 3 * KS) + TILE, F32),
-            pltpu.VMEM((12, KS, 2) + TILE, F32),
+            pltpu.VMEM((9, KS, 2) + TILE, F32),
             pltpu.VMEM((KS, 2) + TILE, F32),
             pltpu.VMEM((2, 16) + TILE, F32),
             pltpu.VMEM((2, 4) + TILE, jnp.int32),
@@ -597,12 +637,16 @@
             pltpu.VMEM((2, 2, 1, BR), F32),
             pltpu.VMEM((KS, 2, 2) + TILE, F32),
             pltpu.VMEM((8, 2) + TILE, F32),
+            pltpu.VMEM((KS, 2) + TILE, F32),
+            pltpu.VMEM((8,) + TILE, F32),
+            pltpu.VMEM((KS, 2) + TILE, F32),
+            pltpu.VMEM((8,) + TILE, F32),
             DMA((6,)),
             DMA,
             DMA((TPD, 8)),
             DMA((TPD, 8)),
             DMA,
-            DMA((2,)),
+            DMA((2, 4)),
             DMA,
             DMA((3,)),
             DMA,
@@ -616,8 +660,8 @@
             DMA((3,)),
             DMA((2, 3)),
             DMA((2, 3)),
-            DMA,
-            DMA,
+            DMA((3,)),
+            DMA((3,)),
         ],
         compiler_params=pltpu.CompilerParams(
             collective_id=0, has_side_effects=True, vmem_limit_bytes=60 * 1024 * 1024

time: 104 us -> 98.5 us (0.947)
  Pallas kernels: 100 us -> 95 us
    pallas_call x1, Pallas kernels: 100 us -> 95 us  [per_device(): pl.pallas_call(kernel, out_shape=[jax.ShapeDtypeStruct((ROWS, 1024), F32)...]
where the time goes in v4:
time: 98.5 us; the launch traced here: 98.3 us
  Pallas kernels  95 us (96%)
  local copies, waits for them, and re-layouts  2 us (2%)
  between operations  1.29 us (1%)
    pallas_call x1, Pallas kernels, per_device(): pl.pallas_call(kernel, out_shape=[jax.ShapeDtypeStruct((ROWS, 1024), F32)...  95 us
    unnamed x4, local copies, waits for them, and re-layouts  2 us

profile of v4, /device:TPU:1, one launch (start us, length us, event | category | flops | bytes accessed | tf_op | source)
XLA Modules:
  0.0 98.3 jit_solution(4002132990409437330)
XLA Ops:
  1.3 95.0 %shard_map.77 = (f32[8,1024]{1,0:T(8,128)}, f32[8,1024]{1,0:T(8,128)}) custom-call(f32[8,8192]{1,0:T(8,128)} %start_hbm.1, f32[8,8192]{1,0:T(8,128)} %diag_hbm.1, f32[3,8,8]{2,1,0:T(8,128)} %left_hbm.1, f32[3,128,128]{2,1,0:T(8,128)} %right_hbm.1, s32[3]{0:T(128)} %shift_hbm.1, s32[1]{0:T(128)S(6)} %copy.10.length_hbm), custom_call_target="tpu_custom_call" | custom-call | flops 600000000 | bytes 2000000 | tf_op jit(solution)/shard_map/pallas_call | solution.py:605
  96.3 0.0 copy-start
  96.3 1.4 %copy.11 = f32[8,1024]{1,0:T(8,128)} copy(f32[8,1024]{1,0:T(8,128)} %get-tuple-element.4) | data formatting | bytes 65536
  97.7 0.0 copy-done
  97.7 0.6 copy.12
Async XLA Ops:
  96.3 1.4 %copy-start = (f32[8,1024]{1,0:T(8,128)S(1)}, f32[8,1024]{1,0:T(8,128)}, u32[]{:S(2)}) copy-start(f32[8,1024]{1,0:T(8,128)} %get-tuple-element.5) | copy-start | bytes 98308

commit v5 on v4

--- a/solution.py
+++ b/solution.py
@@ -72,6 +72,8 @@
     z_send,
     z_plus,
     z_minus,
+    opp_send,
+    opp_recv,
     r_send,
     r_recv,
     x_send,
@@ -125,7 +127,7 @@
         return 4 * lax.rem(y + 4 - o % 4, 4) + lax.rem(x + 4 - o // 4, 4)
 
     loads = [
-        pltpu.make_async_copy(right_hbm, zbuf.at[z], in_sem.at[0]),
+        pltpu.make_async_copy(right_hbm, zbuf.at[z, pl.ds(0, TPD)], in_sem.at[0]),
         pltpu.make_async_copy(start_hbm, start_ref, in_sem.at[1]),
         pltpu.make_async_copy(diag_hbm, diag_ref, in_sem.at[2]),
         pltpu.make_async_copy(left_hbm, left_ref, in_sem.at[3]),
@@ -135,7 +137,9 @@
     for load in loads:
         load.start()
     barrier = pltpu.get_barrier_semaphore()
-    partners = [up, down, other] + [peer(o) for o in offsets]
+    ydevs = [dev(x, lax.rem(y + d, 4), z, c) for d in range(1, 4)]
+    xdevs = [dev(lax.rem(x + d, 4), y, z, c) for d in range(1, 4)]
+    partners = [up, down, other] + xdevs + ydevs
     partners += [dev(x, lax.rem(y + d, 4), z, 1 - c) for d in range(1, 4)]
     for p in partners:
         pl.semaphore_signal(barrier, inc=1, device_id=p, device_id_type=MESH)
@@ -149,32 +153,50 @@
     left_all[c, here, :, TPD * ROWS : TPD * ROWS + 1] = jnp.full((ROWS, 1), length_ref[0].astype(F32), F32)
     shift_all[c, y] = jnp.where(sub == 0, shift_ref[0], jnp.where(sub == 1, shift_ref[1], shift_ref[2]))
     live0 = jnp.where(sub < length_ref[0], 1.0, 0.0).astype(F32)
-    loads[1].wait()
-    loads[2].wait()
+    for load in loads[1:3]:
+        load.wait()
     for m in range(NBLK):
         gd[x, m % 16, m // 16, 0] = start_ref[:, m * BR : (m + 1) * BR] * live0
         gd[x, m % 16, m // 16, 1] = diag_ref[:, m * BR : (m + 1) * BR]
     loads[0].wait()
     pl.semaphore_wait(barrier, len(partners))
 
-    def deliver(zz, t):
+    kind = lax.rem(z - y + 4, 4)
+
+    def is_kind(i, which):
+        return lax.rem(kind + i + NZ, 4) == which
+
+    def deliver(zz, u):
         nn = lax.rem(lax.div(zz, 4), 2)
         yd, cd = lax.rem(zz, 4), lax.div(zz, 8)
-        dst = rbuf.at[nn, y, c, t]
-        sem = r_recv.at[nn, lax.rem(yd - y + 4, 4)]
+        if u < TPD:
+            dst, sem = rbuf.at[nn, y, c, u], r_recv.at[nn, lax.rem(yd - y + 4, 4)]
+        else:
+            dst, sem = rbuf.at[nn, lax.rem(y + 2, 4), c, u - TPD], r_recv.at[nn, 2]
         stays = jnp.logical_and(yd == y, cd == c)
 
         @pl.when(stays)
         def _():
-            pltpu.make_async_copy(zbuf.at[zz, t], dst, sem).start()
+            pltpu.make_async_copy(zbuf.at[zz, u], dst, sem).start()
 
         @pl.when(jnp.logical_not(stays))
         def _():
-            send(zbuf.at[zz, t], dst, r_send, sem, dev(x, yd, z, cd))
-
-    for t in range(TPD):
-        send(zbuf.at[z, t], zbuf.at[z, t], z_send, z_plus.at[t, 0], up)
-        send(zbuf.at[z, t], zbuf.at[z, t], z_send, z_minus.at[t, 0], down)
+            send(zbuf.at[zz, u], dst, r_send, sem, dev(x, yd, z, cd))
+
+    def first_sends(u):
+        send(zbuf.at[z, u], zbuf.at[z, u], z_send, z_plus.at[u, 0], up)
+        send(zbuf.at[z, u], zbuf.at[z, u], z_send, z_minus.at[u, 0], down)
+
+    @pl.when(is_kind(0, 2))
+    def _():
+        for t in range(TPD):
+            send(zbuf.at[z, t], zbuf.at[z, TPD + t], opp_send, opp_recv.at[t], dev(x, lax.rem(y + 2, 4), z, c))
+
+    @pl.when(jnp.logical_not(is_kind(0, 2)))
+    def _():
+        for t in range(TPD):
+            first_sends(t)
+            deliver(z, t)
 
     def half(k, cc):
         return gd.at[k, :, pl.ds(2 * cc, 2)]
@@ -184,47 +206,75 @@
         for d in (2, 1, 3):
             send(rows, rows, x_send, x_recv.at[d - 1], dev(lax.rem(x + d, 4), y, z, c))
 
-    for d in range(1, 4):
-        send(shift_all.at[c, y], shift_all.at[c, y], s_send.at[0], s_recv.at[0], dev(x, lax.rem(y + d, 4), z, c))
-    for o in offsets:
-        send(left_all.at[c, here], left_all.at[c, here], l_send.at[0], l_recv.at[0], peer(o))
-    for t in range(TPD):
-        deliver(z, t)
-
-    def ring_step(i, t):
+    for d in range(3):
+        send(shift_all.at[c, y], shift_all.at[c, y], s_send.at[0], s_recv.at[0], ydevs[d])
+        send(left_all.at[c, here], left_all.at[c, here], l_send.at[0], l_recv.at[0], xdevs[d])
+
+    def send_opposite():
+        @pl.when(is_kind(0, 0))
+        def _():
+            for u in range(TPD, 2 * TPD):
+                wait(zbuf.at[z, u], opp_recv.at[u - TPD])
+                first_sends(u)
+                deliver(z, u)
+
+    def ring_step(i, u):
         zp, zm = lax.rem(z + NZ - i, NZ), lax.rem(z + i, NZ)
         top, low = pl.ds(0, BR // 2), pl.ds(BR // 2, BR // 2)
+
+        def has(j):
+            return is_kind(j, 0) if u >= TPD else jnp.logical_not(is_kind(j, 2))
+
         if i < 8:
-            wait(zbuf.at[zp, t], z_plus.at[t, i - 1])
-            block = zbuf.at[zp, t] if i < 7 else zbuf.at[zp, t, top]
-            send(block, block, z_send, z_plus.at[t, i], up)
-            wait(zbuf.at[zm, t], z_minus.at[t, i - 1])
-            block = zbuf.at[zm, t] if i < 7 else zbuf.at[zm, t, low]
-            send(block, block, z_send, z_minus.at[t, i], down)
-            deliver(zp, t)
-            deliver(zm, t)
+
+            @pl.when(has(-i))
+            def _():
+                wait(zbuf.at[zp, u], z_plus.at[u, i - 1])
+                block = zbuf.at[zp, u] if i < 7 else zbuf.at[zp, u, top]
+                send(block, block, z_send, z_plus.at[u, i], up)
+
+            @pl.when(has(i))
+            def _():
+                wait(zbuf.at[zm, u], z_minus.at[u, i - 1])
+                block = zbuf.at[zm, u] if i < 7 else zbuf.at[zm, u, low]
+                send(block, block, z_send, z_minus.at[u, i], down)
+                deliver(zm, u)
+
+            @pl.when(has(-i))
+            def _():
+                deliver(zp, u)
+
         else:
-            wait(zbuf.at[zp, t, top], z_plus.at[t, 7])
-            wait(zbuf.at[zp, t, low], z_minus.at[t, 7])
-            deliver(zp, t)
+
+            @pl.when(has(0))
+            def _():
+                wait(zbuf.at[zp, u, top], z_plus.at[u, 7])
+                wait(zbuf.at[zp, u, low], z_minus.at[u, 7])
+                deliver(zp, u)
 
     def pass_rows(d):
         k = lax.rem(x + 4 - d, 4)
         wait(half(k, c), x_recv.at[d - 1])
         send(half(k, c), half(k, c), x_send, x_core, other)
 
+    def pass_left():
+        wait(left_all.at[c, pl.ds(0, 3)], l_recv.at[0])
+        row = left_all.at[c, pl.ds(4 * y, 4)]
+        for d in range(3):
+            send(row, row, l_send.at[1], l_recv.at[1], ydevs[d])
+
     def pass_small():
         wait(shift_all.at[c, pl.ds(0, 3)], s_recv.at[0])
         send(shift_all.at[c], shift_all.at[c], s_send.at[1], s_recv.at[1], other)
-        wait(left_all.at[c, pl.ds(0, 15)], l_recv.at[0])
-        send(left_all.at[c], left_all.at[c], l_send.at[1], l_recv.at[1], other)
+        wait(left_all.at[c, pl.ds(0, 12)], l_recv.at[1])
+        send(left_all.at[c], left_all.at[c], l_send.at[2], l_recv.at[2], other)
 
     to_sm = pltpu.make_async_copy(shift_all, shift_sm, sm_sem)
 
     def take_small():
         wait(shift_all.at[1 - c], s_recv.at[1])
         to_sm.start()
-        wait(left_all.at[1 - c], l_recv.at[1])
+        wait(left_all.at[1 - c], l_recv.at[2])
         for k in range(KS):
             length = jnp.broadcast_to(left_all[c, 4 * y + k][:, TPD * ROWS : TPD * ROWS + 1], TILE)
             mask[k] = jnp.where(sub.astype(F32) < length, 1.0, 0.0).astype(F32)
@@ -316,6 +366,7 @@
             y_sum[nn, pl.ds(0, nk)] = acc.reshape((nk,) + TILE)
 
     tasks = {i: [lambda i=i: send_rows(i)] for i in range(8)}
+    tasks[2].append(pass_left)
     tasks[4].append(pass_small)
     tasks[6].append(take_small)
     for i in range(4):
@@ -334,6 +385,14 @@
             ring_step(i, t)
             for task in tasks.get((i - 1) * TPD + t, []):
                 task()
+        for t in range(TPD):
+            if i == 1:
+                continue
+            ring_step(i - 1, TPD + t)
+        if i == 1:
+            send_opposite()
+    for t in range(TPD):
+        ring_step(8, TPD + t)
 
     for nn in range(2):
         for k in range(KS):
@@ -583,11 +642,17 @@
         basis_ref[:, i * BR : (i + 1) * BR] = basis
         image_ref[:, i * BR : (i + 1) * BR] = image
 
-    wait(zbuf.at[pl.ds(0, 15)], z_send)
-    wait(zbuf.at[pl.ds(0, 14)], r_send)
+    wait(zbuf.at[pl.ds(0, 15), pl.ds(0, TPD)], z_send)
+    wait(zbuf.at[pl.ds(0, 12), pl.ds(0, TPD)], r_send)
+
+    @pl.when(is_kind(0, 2))
+    def _():
+        wait(zbuf.at[0, pl.ds(0, TPD)], opp_send)
+
     wait(gd.at[pl.ds(0, 3)], x_send)
-    wait(left_all.at[c, pl.ds(0, 15)], l_send.at[0])
-    wait(left_all.at[c], l_send.at[1])
+    wait(left_all.at[c, pl.ds(0, 3)], l_send.at[0])
+    wait(left_all.at[c, pl.ds(0, 12)], l_send.at[1])
+    wait(left_all.at[c], l_send.at[2])
     wait(shift_all.at[c, pl.ds(0, 3)], s_send.at[0])
     wait(shift_all.at[c], s_send.at[1])
     for ag in (ag2, ag2b, ag3):
@@ -613,7 +678,7 @@
             pltpu.VMEM((TPD, ROWS, ROWS), F32),
             pltpu.SMEM((TPD,), jnp.int32),
             pltpu.SMEM((1,), jnp.int32),
-            pltpu.VMEM((NZ, TPD, BR, BR), F32),
+            pltpu.VMEM((NZ, 2 * TPD, BR, BR), F32),
             pltpu.VMEM((2, 4, 2, TPD, BR, BR), F32),
             pltpu.VMEM((2, 4, 2, TPD, BR, BR), BF16),
             pltpu.VMEM((2, 4, 2, TPD, BR, BR), BF16),
@@ -643,15 +708,17 @@
             pltpu.VMEM((8,) + TILE, F32),
             DMA((6,)),
             DMA,
-            DMA((TPD, 8)),
-            DMA((TPD, 8)),
+            DMA((2 * TPD, 8)),
+            DMA((2 * TPD, 8)),
+            DMA,
+            DMA((TPD,)),
             DMA,
             DMA((2, 4)),
             DMA,
             DMA((3,)),
             DMA,
-            DMA((2,)),
-            DMA((2,)),
+            DMA((3,)),
+            DMA((3,)),
             DMA((2,)),
             DMA((2,)),
             DMA,

time: 98.5 us -> 96.8 us (0.983)
  Pallas kernels: 95 us -> 93.3 us
    pallas_call x1, Pallas kernels: 95 us -> 93.3 us  [per_device(): pl.pallas_call(kernel, out_shape=[jax.ShapeDtypeStruct((ROWS, 1024), F32)...]
where the time goes in v5:
time: 96.8 us; the launch traced here: 96.6 us
  Pallas kernels  93.3 us (96%)
  local copies, waits for them, and re-layouts  2 us (2%)
  between operations  1.29 us (1%)
    pallas_call x1, Pallas kernels, per_device(): pl.pallas_call(kernel, out_shape=[jax.ShapeDtypeStruct((ROWS, 1024), F32)...  93.3 us
    unnamed x4, local copies, waits for them, and re-layouts  2 us

profile of v5, /device:TPU:1, one launch (start us, length us, event | category | flops | bytes accessed | tf_op | source)
XLA Modules:
  0.0 96.6 jit_solution(10134623129337219895)
XLA Ops:
  1.3 93.3 %shard_map.77 = (f32[8,1024]{1,0:T(8,128)}, f32[8,1024]{1,0:T(8,128)}) custom-call(f32[8,8192]{1,0:T(8,128)} %start_hbm.1, f32[8,8192]{1,0:T(8,128)} %diag_hbm.1, f32[3,8,8]{2,1,0:T(8,128)} %left_hbm.1, f32[3,128,128]{2,1,0:T(8,128)} %right_hbm.1, s32[3]{0:T(128)} %shift_hbm.1, s32[1]{0:T(128)S(6)} %copy.10.length_hbm), custom_call_target="tpu_custom_call" | custom-call | flops 600000000 | bytes 2000000 | tf_op jit(solution)/shard_map/pallas_call | solution.py:670
  94.6 0.0 copy-start
  94.6 1.4 %copy.11 = f32[8,1024]{1,0:T(8,128)} copy(f32[8,1024]{1,0:T(8,128)} %get-tuple-element.4) | data formatting | bytes 65536
  96.0 0.0 copy-done
  96.0 0.6 copy.12
Async XLA Ops:
  94.6 1.4 %copy-start = (f32[8,1024]{1,0:T(8,128)S(1)}, f32[8,1024]{1,0:T(8,128)}, u32[]{:S(2)}) copy-start(f32[8,1024]{1,0:T(8,128)} %get-tuple-element.5) | copy-start | bytes 98308

commit v6 on v5

--- a/solution.py
+++ b/solution.py
@@ -61,7 +61,6 @@
     d_rows,
     dz,
     dp,
-    dc,
     qs_src,
     qs_got,
     t_src,
@@ -120,8 +119,8 @@
     zdevs = [dev(x, y, lax.rem(z + d, NZ), c) for d in range(1, NZ)]
     offsets = sorted(range(1, 16), key=lambda o: -(min(o // 4, 4 - o // 4) + min(o % 4, 4 - o % 4)))
 
-    def peer(o):
-        return dev(lax.rem(x + o // 4, 4), lax.rem(y + o % 4, 4), z, c)
+    def peer(o, core=c):
+        return dev(lax.rem(x + o // 4, 4), lax.rem(y + o % 4, 4), z, core)
 
     def sender(o):
         return 4 * lax.rem(y + 4 - o % 4, 4) + lax.rem(x + 4 - o // 4, 4)
@@ -406,11 +405,11 @@
         def at(r, cc):
             return v.at[:, r, pl.ds(2 * cc, 2)]
 
-        def start(nn):
-            half = v.at[:, here, pl.ds(2 * c + nn, 1)]
+        def start(nn=None):
+            own = at(here, c) if nn is None else v.at[:, here, pl.ds(2 * c + nn, 1)]
             for o in offsets:
-                send(half, half, ag_send.at[phase, 0], ag_recv.at[phase, o], peer(o))
-            send(half, half, ag_send.at[phase, 1], ag_core.at[phase], other)
+                send(own, own, ag_send.at[phase, 0], ag_recv.at[phase, o], peer(o))
+            send(own, own, ag_send.at[phase, 1], ag_core.at[phase], other)
 
         def pass_on(first, last):
             for o in offsets[::-1][first:last]:
@@ -441,26 +440,23 @@
 
         def plane():
             wait(dz.at[g, pl.ds(0, 15)], dot_recv.at[g, 0])
-            dp[g, here] = jnp.sum(dz[g], axis=0)
+            own = dp.at[g, 16 * c + here]
+            dp[g, 16 * c + here] = jnp.sum(dz[g], axis=0)
             for o in offsets:
-                send(dp.at[g, here], dp.at[g, here], dot_send.at[g, 1], dot_recv.at[g, 1], peer(o))
-
-        def core():
-            wait(dp.at[g, pl.ds(0, 15)], dot_recv.at[g, 1])
-            dc[g, c] = jnp.sum(dp[g], axis=0)
-            send(dc.at[g, c], dc.at[g, c], dot_send.at[g, 2], dot_recv.at[g, 2], other)
+                send(own, own, dot_send.at[g, 1], dot_recv.at[g, 1], peer(o))
+                send(own, own, dot_send.at[g, 1], dot_recv.at[g, 1], peer(o, 1 - c))
+            send(own, own, dot_send.at[g, 1], dot_recv.at[g, 1], other)
 
         def done(pairs):
-            wait(dc.at[g, 1 - c], dot_recv.at[g, 2])
-            total = dc[g, 0] + dc[g, 1]
+            wait(dp.at[g, pl.ds(0, 31)], dot_recv.at[g, 1])
+            total = jnp.sum(dp[g], axis=0)
             return {p: jnp.broadcast_to(total[:, r : r + 1], TILE) for r, p in enumerate(pairs)}
 
         def sent():
             wait(dz.at[g, pl.ds(0, 15)], dot_send.at[g, 0])
-            wait(dp.at[g, pl.ds(0, 15)], dot_send.at[g, 1])
-            wait(dc.at[g, c], dot_send.at[g, 2])
-
-        return start, plane, core, done, sent
+            wait(dp.at[g, pl.ds(0, 31)], dot_send.at[g, 1])
+
+        return start, plane, done, sent
 
     spot = 4 * lax.rem(y, 2) + x
     cd = lax.div(y, 2)
@@ -522,15 +518,13 @@
     early[0](EARLY)
     ag2[1](0, 10)
     early[1]()
-    ag2b[0](0)
-    ag2b[0](1)
+    ag2b[0]()
     ex_early[0]()
     ag2[1](10, 15)
     ag2[2]()
 
     product(v2, KS)
-    early[2]()
-    dot = early[3](EARLY)
+    dot = early[2](EARLY)
     f1 = jnp.sqrt(CELLS / (dot[G, G] + EPS))
     r1 = f1 * f1 * dot[G, H_] / CELLS
     for nn in range(2):
@@ -539,7 +533,7 @@
             piece[PP, k, nn] = pp
             piece[AP, k, nn] = pp * inv[k, nn]
             v3[k, here, 2 * c + nn] = pp * inv[k, nn]
-        ag3[0](nn)
+    ag3[0]()
     late[0](LATE)
     ag2b[1](0, 15)
     ag2b[2]()
@@ -558,8 +552,7 @@
         for k in range(KS):
             o_src[k, nn] = y_sum[nn, k] * mask[k]
     ex_o[0]()
-    late[2]()
-    dot.update(late[3](LATE))
+    dot.update(late[2](LATE))
     dot.update({(b, a): value for (a, b), value in dot.items()})
 
     c1 = f1 * f1 * (dot[G, A_] - r1 * dot[G, B]) / CELLS
@@ -657,8 +650,8 @@
     wait(shift_all.at[c], s_send.at[1])
     for ag in (ag2, ag2b, ag3):
         ag[3]()
-    early[4]()
-    late[4]()
+    early[3]()
+    late[3]()
     for ex in (ex_early, ex_t, ex_o):
         ex[2]()
 
@@ -698,8 +691,7 @@
             pltpu.VMEM((KS,) + TILE, F32),
             pltpu.VMEM((2, 16, BR), F32),
             pltpu.VMEM((2, 16, 1, BR), F32),
-            pltpu.VMEM((2, 16, 1, BR), F32),
-            pltpu.VMEM((2, 2, 1, BR), F32),
+            pltpu.VMEM((2, 32, 1, BR), F32),
             pltpu.VMEM((KS, 2, 2) + TILE, F32),
             pltpu.VMEM((8, 2) + TILE, F32),
             pltpu.VMEM((KS, 2) + TILE, F32),
@@ -725,8 +717,8 @@
             DMA((3, 2)),
             DMA((3, 16)),
             DMA((3,)),
-            DMA((2, 3)),
-            DMA((2, 3)),
+            DMA((2, 2)),
+            DMA((2, 2)),
             DMA((3,)),
             DMA((3,)),
         ],

time: 96.8 us -> 95.8 us (0.990)
  Pallas kernels: 93.3 us -> 92.3 us
    pallas_call x1, Pallas kernels: 93.3 us -> 92.3 us  [per_device(): pl.pallas_call(kernel, out_shape=[jax.ShapeDtypeStruct((ROWS, 1024), F32)...]
where the time goes in v6:
time: 95.8 us; the launch traced here: 95.6 us
  Pallas kernels  92.3 us (96%)
  local copies, waits for them, and re-layouts  2 us (2%)
  between operations  1.29 us (1%)
    pallas_call x1, Pallas kernels, per_device(): pl.pallas_call(kernel, out_shape=[jax.ShapeDtypeStruct((ROWS, 1024), F32)...  92.3 us
    unnamed x4, local copies, waits for them, and re-layouts  2 us

profile of v6, /device:TPU:1, one launch (start us, length us, event | category | flops | bytes accessed | tf_op | source)
XLA Modules:
  0.0 95.6 jit_solution(17934491586183991136)
XLA Ops:
  1.3 92.3 %shard_map.77 = (f32[8,1024]{1,0:T(8,128)}, f32[8,1024]{1,0:T(8,128)}) custom-call(f32[8,8192]{1,0:T(8,128)} %start_hbm.1, f32[8,8192]{1,0:T(8,128)} %diag_hbm.1, f32[3,8,8]{2,1,0:T(8,128)} %left_hbm.1, f32[3,128,128]{2,1,0:T(8,128)} %right_hbm.1, s32[3]{0:T(128)} %shift_hbm.1, s32[1]{0:T(128)S(6)} %copy.10.length_hbm), custom_call_target="tpu_custom_call" | custom-call | flops 600000000 | bytes 2000000 | tf_op jit(solution)/shard_map/pallas_call | solution.py:663
  93.6 0.0 copy-start
  93.6 1.4 %copy.11 = f32[8,1024]{1,0:T(8,128)} copy(f32[8,1024]{1,0:T(8,128)} %get-tuple-element.4) | data formatting | bytes 65536
  95.0 0.0 copy-done
  95.0 0.6 copy.12
Async XLA Ops:
  93.6 1.4 %copy-start = (f32[8,1024]{1,0:T(8,128)S(1)}, f32[8,1024]{1,0:T(8,128)}, u32[]{:S(2)}) copy-start(f32[8,1024]{1,0:T(8,128)} %get-tuple-element.5) | copy-start | bytes 98308

commit v7 on v6

--- a/solution.py
+++ b/solution.py
@@ -356,13 +356,15 @@
             acc = res if acc is None else acc + res
         return acc
 
-    def product(v, nk):
+    def product(v, nk, after=None):
         mix(v, nk, 0, TERMS, 4)
         for nn in range(2):
             acc = terms_of(nn, 0, nk * ROWS, False)
             for yy in range(1, 4):
                 acc = acc + terms_of(nn, yy, nk * ROWS, False)
             y_sum[nn, pl.ds(0, nk)] = acc.reshape((nk,) + TILE)
+            if after is not None:
+                after(nn)
 
     tasks = {i: [lambda i=i: send_rows(i)] for i in range(8)}
     tasks[2].append(pass_left)
@@ -463,9 +465,9 @@
     keeps = cd == c
 
     def exchange(i, src, got):
-        def start():
+        def start(blocks=(0, 1)):
             for k in range(KS):
-                for nn in range(2):
+                for nn in blocks:
                     stays = jnp.logical_and(jnp.logical_and(x == k, y == 2 * c + nn), keeps)
 
                     @pl.when(stays)
@@ -547,11 +549,12 @@
     ag3[1](10, 15)
     ag3[2]()
 
-    product(v3, KS)
-    for nn in range(2):
+    def hand_over(nn):
         for k in range(KS):
             o_src[k, nn] = y_sum[nn, k] * mask[k]
-    ex_o[0]()
+        ex_o[0]((nn,))
+
+    product(v3, KS, hand_over)
     dot.update(late[2](LATE))
     dot.update({(b, a): value for (a, b), value in dot.items()})
 

time: 95.8 us -> 95.8 us (level)
  no operation moved by 1% of the time
where the time goes in v7:
time: 95.8 us; the launch traced here: 95.6 us
  Pallas kernels  92.3 us (96%)
  local copies, waits for them, and re-layouts  2 us (2%)
  between operations  1.29 us (1%)
    pallas_call x1, Pallas kernels, per_device(): pl.pallas_call(kernel, out_shape=[jax.ShapeDtypeStruct((ROWS, 1024), F32)...  92.3 us
    unnamed x4, local copies, waits for them, and re-layouts  2 us

profile of v7, /device:TPU:1, one launch (start us, length us, event | category | flops | bytes accessed | tf_op | source)
XLA Modules:
  0.0 95.6 jit_solution(10563760475289848221)
XLA Ops:
  1.3 92.3 %shard_map.77 = (f32[8,1024]{1,0:T(8,128)}, f32[8,1024]{1,0:T(8,128)}) custom-call(f32[8,8192]{1,0:T(8,128)} %start_hbm.1, f32[8,8192]{1,0:T(8,128)} %diag_hbm.1, f32[3,8,8]{2,1,0:T(8,128)} %left_hbm.1, f32[3,128,128]{2,1,0:T(8,128)} %right_hbm.1, s32[3]{0:T(128)} %shift_hbm.1, s32[1]{0:T(128)S(6)} %copy.10.length_hbm), custom_call_target="tpu_custom_call" | custom-call | flops 600000000 | bytes 2000000 | tf_op jit(solution)/shard_map/pallas_call | solution.py:666
  93.6 0.0 copy-start
  93.6 1.4 %copy.11 = f32[8,1024]{1,0:T(8,128)} copy(f32[8,1024]{1,0:T(8,128)} %get-tuple-element.4) | data formatting | bytes 65536
  95.0 0.0 copy-done
  95.0 0.6 copy.12
Async XLA Ops:
  93.6 1.4 %copy-start = (f32[8,1024]{1,0:T(8,128)S(1)}, f32[8,1024]{1,0:T(8,128)}, u32[]{:S(2)}) copy-start(f32[8,1024]{1,0:T(8,128)} %get-tuple-element.5) | copy-start | bytes 98308
